TPU v7x, 1024 devices: a whole 4x8x16 slice. The times are simulated.
1024 devices in a mesh: pipe: 4 (over x), expert: 64 (over y_hi, z, core), dp: 4 (over y_lo).
Axes of the slice: x: 4, y: 8 (y_hi: 2, y_lo: 4; y = y_hi * 4 + y_lo), z: 16, core: 2. Of those that a mesh axis runs over, the one named last changes fastest.
Arguments:
- x_fwd: bfloat16 [4, 2048, 3584], P('pipe', ('expert', 'dp')), may hold values from -6 to 6
- ids_fwd: int32 [4, 2048, 2], P('pipe', ('expert', 'dp')), may hold values from 0 to 15, all different within a row; in each aligned block of 8 rows (0 to 7, 8 to 15, ..., all dimensions but the last counted through in order) at most 2 rows name the same one
- prob_fwd: float32 [4, 2048, 2], P('pipe', ('expert', 'dp')), may hold values from 0.2 to 1
- grad_bwd: bfloat16 [4, 2048, 3584], P('pipe', ('expert', 'dp')), may hold values from -1.796875 to 1.796875
- ids_bwd: int32 [4, 2048, 2], P('pipe', ('expert', 'dp')), may hold values from 0 to 15, all different within a row; in each aligned block of 8 rows (0 to 7, 8 to 15, ..., all dimensions but the last counted through in order) at most 2 rows name the same one
- prob_bwd: float32 [4, 2048, 2], P('pipe', ('expert', 'dp')), may hold values from 0.2 to 1
- pre_bwd: bfloat16 [4, 2048, 2, 2, 1024], P('pipe', ('expert', 'dp')), may hold values from -6 to 6
- w_gate: bfloat16 [4, 3584, 16384], P('pipe', None, 'expert'), may hold values from -0.09375 to 0.09375
- w_up: bfloat16 [4, 3584, 16384], P('pipe', None, 'expert'), may hold values from -0.09375 to 0.09375
- w_down: bfloat16 [4, 16384, 3584], P('pipe', 'expert'), may hold values from -0.375 to 0.375
Outputs:
- next_input: bfloat16 [4, 2048, 3584], P('pipe', ('expert', 'dp'))
- grad_input: bfloat16 [4, 2048, 3584], P('pipe', ('expert', 'dp'))
- grad_down: float32 [4, 16384, 3584], P('pipe', ('expert', 'dp'))
Inputs may be any that keep to these rules, and one draw needn't show every extreme that they name: `ids_fwd`: in each aligned block of 8 rows (the tokens of one device) no expert is named by more than 2 rows, a bound that some block reaches. `ids_bwd`: same bound per aligned block of 8 rows as for the forward routes.
All inputs are finite; a program needn't handle non-finite values.
Results may differ from a plain program's by a relative error of at most 0.011.
Values may be sent and summed in bfloat16 or wider, within the bound.
No kernel may reach another device: no remote copies, remote signals or barrier semaphores. Data moves between devices by JAX's collectives and lax.ppermute only.
A program may use at most 32 MiB of HBM per device.

v0:
```python
import jax
import jax.numpy as jnp
from jax import lax
from jax.sharding import PartitionSpec as P


def shifted(block, axis, distance):
    devices = range(lax.axis_size(axis))
    route = [((i - distance) % len(devices), i) for i in devices]
    return lax.ppermute(block, axis, route)


def silu_pair(value):
    sig = jax.nn.sigmoid(value)
    return (value * sig, sig * (1.0 + value * (1.0 - sig)))


def route_tables(route_ids, route_probs, experts, slots):
    tokens, chosen = route_ids.shape
    pairs = route_ids.reshape(-1)
    labels = jnp.arange(experts, dtype=jnp.int32)
    onehot = (pairs[:, None] == labels[None, :]).astype(jnp.int32)
    before = jnp.cumsum(onehot, axis=0) - onehot
    slot_of = jnp.sum(onehot * before, axis=1)
    position = pairs * slots + slot_of
    places = jnp.arange(experts * slots, dtype=jnp.int32)
    select = (position[None, :] == places[:, None]).astype(jnp.float32)
    weighted = select * route_probs.reshape(-1)[None, :]
    by_token = jnp.sum(select.reshape(experts * slots, tokens, chosen), axis=2)
    weighted_token = jnp.sum(weighted.reshape(experts * slots, tokens, chosen), axis=2)
    return (select, by_token, weighted_token)


def fan_out(rows, experts, shards, slots):
    width = rows.shape[-1]
    grouped = rows.reshape(experts, 1, slots, width)
    return jnp.broadcast_to(grouped, (experts, shards, slots, width)).reshape(
        experts * shards, slots, width
    )


def forward_experts(rows, wg_local, wu_local, wd_local):
    flat = rows.reshape(-1, rows.shape[-1])
    gate_pre = jnp.dot(flat, wg_local, preferred_element_type=jnp.float32)
    up_pre = jnp.dot(flat, wu_local, preferred_element_type=jnp.float32)
    act, _ = silu_pair(gate_pre)
    hidden = (act * up_pre).astype(jnp.bfloat16)
    out_rows = jnp.dot(hidden, wd_local, preferred_element_type=jnp.float32).astype(jnp.bfloat16)
    return out_rows.reshape(rows.shape)


def backward_experts(grads, pre_rows, wg_local, wu_local, wd_local):
    units = wg_local.shape[1]
    flat_g = grads.reshape(-1, grads.shape[-1])
    flat_pre = pre_rows.reshape(-1, 2 * units).astype(jnp.float32)
    gate_pre = flat_pre[:, :units]
    up_pre = flat_pre[:, units:]
    act, slope = silu_pair(gate_pre)
    hidden = (act * up_pre).astype(jnp.bfloat16)
    contract = (((1,), (1,)), ((), ()))
    dhid = lax.dot_general(flat_g, wd_local, contract, preferred_element_type=jnp.float32)
    d_gate = (dhid * up_pre * slope).astype(jnp.bfloat16)
    d_up = (dhid * act).astype(jnp.bfloat16)
    dx_rows = lax.dot_general(d_gate, wg_local, contract, preferred_element_type=jnp.float32)
    dx_rows = dx_rows + lax.dot_general(
        d_up, wu_local, contract, preferred_element_type=jnp.float32
    )
    return (dx_rows.astype(jnp.bfloat16).reshape(grads.shape), hidden, flat_g)


def reduce_grad(hidden, flat_g):
    return lax.psum_scatter(
        lax.dot_general(
            hidden, flat_g, (((0,), (0,)), ((), ())), preferred_element_type=jnp.float32
        ).astype(jnp.bfloat16),
        "dp",
        scatter_dimension=0,
        tiled=True,
    ).astype(jnp.float32)


def gather_back(received, experts, shards, table):
    slots = received.shape[1]
    width = received.shape[2]
    summed = jnp.sum(received.reshape(experts, shards, slots, width), axis=1, dtype=jnp.float32)
    summed = summed.reshape(experts * slots, width)
    return lax.dot_general(
        table,
        summed,
        (((0,), (0,)), ((), ())),
        precision=lax.Precision.HIGHEST,
        preferred_element_type=jnp.float32,
    )


def on_device(x_fwd, ids_fwd, prob_fwd, grad_bwd, ids_bwd, prob_bwd, pre_bwd, w_gate, w_up, w_down):
    devices = lax.axis_size("expert")
    shards = min(4, devices // 2)
    experts = devices // shards
    tokens = x_fwd.shape[1]
    chosen = ids_fwd.shape[2]
    slots = max(2, min(tokens, 2 * ((tokens * chosen + experts - 1) // experts)))
    wg_local = w_gate[0]
    wu_local = w_up[0]
    wd_local = w_down[0]
    units = wg_local.shape[1]
    select_f, token_f, weight_f = route_tables(ids_fwd[0], prob_fwd[0], experts, slots)
    select_b, token_b, weight_b = route_tables(ids_bwd[0], prob_bwd[0], experts, slots)
    send_x = jnp.dot(token_f.astype(jnp.bfloat16), x_fwd[0], preferred_element_type=jnp.float32)
    send_x = fan_out(send_x.astype(jnp.bfloat16), experts, shards, slots)
    send_g = jnp.dot(weight_b, grad_bwd[0].astype(jnp.float32), precision=lax.Precision.HIGHEST)
    send_g = fan_out(send_g.astype(jnp.bfloat16), experts, shards, slots)
    pre_flat = pre_bwd[0].reshape(tokens * chosen, -1)
    pre_rows = jnp.dot(select_b.astype(jnp.bfloat16), pre_flat, preferred_element_type=jnp.float32)
    pre_rows = pre_rows.astype(jnp.bfloat16).reshape(experts, slots, 2, shards, units)
    pre_rows = pre_rows.transpose(0, 3, 1, 2, 4).reshape(devices, slots, 2 * units)
    got_x, got_g, got_pre = (
        lax.all_to_all(send_x, "expert", split_axis=0, concat_axis=0, tiled=True),
        lax.all_to_all(send_g, "expert", split_axis=0, concat_axis=0, tiled=True),
        lax.all_to_all(pre_rows, "expert", split_axis=0, concat_axis=0, tiled=True),
    )
    out_rows = forward_experts(got_x, wg_local, wu_local, wd_local)
    dx_rows, hidden, flat_g = backward_experts(got_g, got_pre, wg_local, wu_local, wd_local)
    back_y, back_dx = (
        lax.all_to_all(out_rows, "expert", split_axis=0, concat_axis=0, tiled=True),
        lax.all_to_all(dx_rows, "expert", split_axis=0, concat_axis=0, tiled=True),
    )
    grad_rows = reduce_grad(hidden, flat_g)
    routed = gather_back(back_y, experts, shards, weight_f).astype(jnp.bfloat16)
    moved = shifted(routed[None], "pipe", 1)
    grad_input = gather_back(back_dx, experts, shards, token_b).astype(jnp.bfloat16)
    return (moved, grad_input[None], grad_rows[None])


def solution(mesh):
    in_specs = (
        P("pipe", ("expert", "dp"), None),
        P("pipe", ("expert", "dp"), None),
        P("pipe", ("expert", "dp"), None),
        P("pipe", ("expert", "dp"), None),
        P("pipe", ("expert", "dp"), None),
        P("pipe", ("expert", "dp"), None),
        P("pipe", ("expert", "dp"), None, None, None),
        P("pipe", None, "expert"),
        P("pipe", None, "expert"),
        P("pipe", "expert", None),
    )
    out_specs = (
        P("pipe", ("expert", "dp"), None),
        P("pipe", ("expert", "dp"), None),
        P("pipe", ("expert", "dp"), None),
    )
    return jax.shard_map(
        on_device, mesh=mesh, in_specs=in_specs, out_specs=out_specs, check_vma=False
    )
```

profile of v0, /device:TPU:1, one launch (start us, length us, event | category | flops | bytes accessed | tf_op | source)
XLA Modules:
  0.0 316.7 jit_solution(1438078544422119013)
XLA Ops:
  7.2 0.0 copy-start
  7.2 0.9 copy.33
  8.1 0.1 eq.73
  8.1 0.1 fusion.34
  8.3 0.2 select_reduce_fusion.1
  8.5 0.9 copy.36
  9.3 0.2 convolution_convert_fusion.6
  9.5 0.1 reshape.128
  9.6 0.1 copy.35
  9.7 0.7 reshape.129
  10.4 26.1 %all-to-all-start.3 = ((bf16[64,2,512]{2,1,0:T(2,128)(2,1)}), bf16[64,2,512]{2,1,0:T(2,128)(2,1)S(1)}, u32[]{:S(2)}, u32[]{:S(2)}) async-start(bf16[64,2,512]{2,1,0:T(2,128)(2,1)} %reshape.129), calls=%async_computation.3 | async-start | bytes 262144 | tf_op jit(solution)/shard_map/all_to_all | solution.py:120
  36.5 0.1 reduce_sum.82
  36.6 0.1 copy.34
  36.7 0.7 bitcast_add_fusion
  37.4 0.8 select_reduce_fusion
  38.1 0.0 copy-start.3
  38.1 1.2 convolution_convert_fusion.2
  39.4 0.1 broadcast_in_dim.35
  39.5 18.1 %all-to-all-done.3 = bf16[64,2,512]{2,1,0:T(2,128)(2,1)S(1)} async-done(((bf16[64,2,512]{2,1,0:T(2,128)(2,1)}), bf16[64,2,512]{2,1,0:T(2,128)(2,1)S(1)}, u32[]{:S(2)}, u32[]{:S(2)}) %all-to-all-start.3) | async-done | bytes 131104 | tf_op jit(solution)/shard_map/all_to_all | solution.py:120
  57.5 1.4 broadcast_in_dim.36
  58.9 4.5 %all-to-all-start.2 = ((bf16[64,2,3584]{2,1,0:T(2,128)(2,1)}), bf16[64,2,3584]{2,1,0:T(2,128)(2,1)S(1)}, u32[]{:S(2)}, u32[]{:S(2)}) async-start(bf16[64,2,3584]{2,1,0:T(2,128)(2,1)} %bitcast.63), calls=%async_computation.2 | async-start | bytes 1835008 | tf_op jit(solution)/shard_map/all_to_all | solution.py:119
  63.4 0.0 copy-done.4
  63.4 0.1 copy.31
  63.5 0.1 eq.66
  63.6 0.1 fusion.35
  63.7 0.2 select_reduce_fusion.3
  63.9 0.1 reduce_sum.77
  64.0 0.1 copy.32
  64.1 0.0 copy-done.5
  64.1 0.1 convert_reduce_fusion.3
  64.2 0.3 convolution_convert_fusion.3
  64.4 0.1 broadcast_in_dim.32
  64.5 48.3 %all-to-all-done.2 = bf16[64,2,3584]{2,1,0:T(2,128)(2,1)S(1)} async-done(((bf16[64,2,3584]{2,1,0:T(2,128)(2,1)}), bf16[64,2,3584]{2,1,0:T(2,128)(2,1)S(1)}, u32[]{:S(2)}, u32[]{:S(2)}) %all-to-all-start.2) | async-done | bytes 917536 | tf_op jit(solution)/shard_map/all_to_all | solution.py:119
  112.8 1.4 broadcast_in_dim.33
  114.2 9.2 %all-to-all-start = ((bf16[64,2,3584]{2,1,0:T(2,128)(2,1)}), bf16[64,2,3584]{2,1,0:T(2,128)(2,1)}, u32[]{:S(2)}, u32[]{:S(2)}) async-start(bf16[64,2,3584]{2,1,0:T(2,128)(2,1)} %bitcast.64), calls=%async_computation | async-start | bytes 1835008 | tf_op jit(solution)/shard_map/all_to_all | solution.py:118
  123.5 2.5 reshape.127
  125.9 0.0 copy-start.1
  125.9 2.3 fusion.3
  128.3 0.7 fusion.9
  129.1 1.7 fusion
  130.7 3.1 reshape.130
  133.8 38.7 %all-to-all-done = bf16[64,2,3584]{2,1,0:T(2,128)(2,1)} async-done(((bf16[64,2,3584]{2,1,0:T(2,128)(2,1)}), bf16[64,2,3584]{2,1,0:T(2,128)(2,1)}, u32[]{:S(2)}, u32[]{:S(2)}) %all-to-all-start) | async-done | bytes 917536 | tf_op jit(solution)/shard_map/all_to_all | solution.py:118
  172.6 9.2 %all-to-all-start.4 = ((bf16[64,2,3584]{2,1,0:T(2,128)(2,1)}), bf16[64,2,3584]{2,1,0:T(2,128)(2,1)}, u32[]{:S(2)}, u32[]{:S(2)}) async-start(bf16[64,2,3584]{2,1,0:T(2,128)(2,1)} %reshape.130), calls=%async_computation.4 | async-start | bytes 1835008 | tf_op jit(solution)/shard_map/all_to_all | solution.py:126
  181.8 3.2 %reshape.123 = bf16[128,3584]{1,0:T(8,128)(2,1)} reshape(bf16[64,2,3584]{2,1,0:T(2,128)(2,1)} %all-to-all-done) | data formatting | bytes 1835008 | tf_op jit(solution)/shard_map/reshape | solution.py:43
  185.0 2.2 fusion.11
  187.2 3.9 %convolution_convert_fusion.1 = bf16[128,3584]{1,0:T(8,128)(2,1)} fusion(bf16[1,256,3584]{2,1,0:T(8,128)(2,1)} %param.19, bf16[128,3584]{1,0:T(8,128)(2,1)} %reshape.123, bf16[1,3584,256]{2,1,0:T(8,128)(2,1)S(1)} %copy-done, f32[128,256]{1,0:T(8,128)S(1)} %fusion.11), kind=kOutput, calls=%fused_computation.3 | convolution fusion | flops 470417408 | bytes 5636096 | tf_op jit(solution)/shard_map/dot_general | solution.py:48
  191.1 3.1 reshape.124
  194.2 36.8 %all-to-all-done.4 = bf16[64,2,3584]{2,1,0:T(2,128)(2,1)} async-done(((bf16[64,2,3584]{2,1,0:T(2,128)(2,1)}), bf16[64,2,3584]{2,1,0:T(2,128)(2,1)}, u32[]{:S(2)}, u32[]{:S(2)}) %all-to-all-start.4) | async-done | bytes 917536 | tf_op jit(solution)/shard_map/all_to_all | solution.py:126
  231.0 9.2 %all-to-all-start.1 = ((bf16[64,2,3584]{2,1,0:T(2,128)(2,1)}), bf16[64,2,3584]{2,1,0:T(2,128)(2,1)}, u32[]{:S(2)}, u32[]{:S(2)}) async-start(bf16[64,2,3584]{2,1,0:T(2,128)(2,1)} %reshape.124), calls=%async_computation.1 | async-start | bytes 1835008 | tf_op jit(solution)/shard_map/all_to_all | solution.py:125
  240.2 0.0 reduce-scatter.2.cloned.1.call-start
  240.2 1.9 convolution_convert_fusion
  242.2 0.0 reduce-scatter.2.cloned.1.call-update
  242.2 2.3 convert_reduce_fusion
  244.5 0.3 reshape.131
  244.8 44.6 %all-to-all-done.1 = bf16[64,2,3584]{2,1,0:T(2,128)(2,1)} async-done(((bf16[64,2,3584]{2,1,0:T(2,128)(2,1)}), bf16[64,2,3584]{2,1,0:T(2,128)(2,1)}, u32[]{:S(2)}, u32[]{:S(2)}) %all-to-all-start.1) | async-done | bytes 917536 | tf_op jit(solution)/shard_map/all_to_all | solution.py:125
  289.4 2.3 convert_reduce_fusion.1
  291.7 0.3 reshape.125
  292.0 0.3 fusion.1
  292.3 3.1 collective-permute-start
  295.5 1.0 fusion.2
  296.4 2.4 collective-permute-done
  298.9 8.4 %reduce-scatter.2.cloned.1.call-done = bf16[64,3584]{1,0:T(8,128)(2,1)} async-done(((bf16[256,3584]{1,0:T(8,128)(2,1)}), bf16[64,3584]{1,0:T(8,128)(2,1)}) %reduce-scatter.2.cloned.1.call-update) | async-done | bytes 458768 | tf_op jit(solution)/shard_map/reduce_scatter | solution.py:72
  307.2 2.0 bitcast_convert_fusion
  309.2 0.6 copy.38
  (12 shorter events, 0.1 us)
Async XLA Ops:
  7.2 121.9 %copy-start = (bf16[1,3584,256]{2,1,0:T(8,128)(2,1)S(1)}, bf16[1,3584,256]{2,1,0:T(8,128)(2,1)}, u32[]{:S(2)}) copy-start(bf16[1,3584,256]{2,1,0:T(8,128)(2,1)} %param.18) | copy-start | bytes 5505028
  10.4 47.1 %all-to-all-start.3 = ((bf16[64,2,512]{2,1,0:T(2,128)(2,1)}), bf16[64,2,512]{2,1,0:T(2,128)(2,1)S(1)}, u32[]{:S(2)}, u32[]{:S(2)}) async-start(bf16[64,2,512]{2,1,0:T(2,128)(2,1)} %reshape.129), calls=%async_computation.3 | async-start | bytes 262144 | tf_op jit(solution)/shard_map/all_to_all | solution.py:120
  38.1 25.3 %copy-start.4 = (s32[1,8,2]{1,2,0:T(2,128)S(1)}, s32[1,8,2]{1,2,0:T(2,128)}, u32[]{:S(2)}) copy-start(s32[1,8,2]{1,2,0:T(2,128)} %param.11) | copy-start | bytes 196
  38.1 26.0 %copy-start.5 = (f32[1,8,2]{1,2,0:T(2,128)S(1)}, f32[1,8,2]{1,2,0:T(2,128)}, u32[]{:S(2)}) copy-start(f32[1,8,2]{1,2,0:T(2,128)} %param.12) | copy-start | bytes 196
  38.1 26.0 %copy-start.3 = (bf16[1,8,3584]{2,1,0:T(8,128)(2,1)S(1)}, bf16[1,8,3584]{2,1,0:T(8,128)(2,1)}, u32[]{:S(2)}) copy-start(bf16[1,8,3584]{2,1,0:T(8,128)(2,1)} %param.10) | copy-start | bytes 172036
  58.9 53.8 %all-to-all-start.2 = ((bf16[64,2,3584]{2,1,0:T(2,128)(2,1)}), bf16[64,2,3584]{2,1,0:T(2,128)(2,1)S(1)}, u32[]{:S(2)}, u32[]{:S(2)}) async-start(bf16[64,2,3584]{2,1,0:T(2,128)(2,1)} %bitcast.63), calls=%async_computation.2 | async-start | bytes 1835008 | tf_op jit(solution)/shard_map/all_to_all | solution.py:119
  112.8 10.6 %copy-start.2 = (bf16[64,2,3584]{2,1,0:T(2,128)(2,1)}, bf16[64,2,3584]{2,1,0:T(2,128)(2,1)S(1)}, u32[]{:S(2)}) copy-start(bf16[64,2,3584]{2,1,0:T(2,128)(2,1)S(1)} %all-to-all-done.2) | copy-start | bytes 2752516
  114.2 58.4 %all-to-all-start = ((bf16[64,2,3584]{2,1,0:T(2,128)(2,1)}), bf16[64,2,3584]{2,1,0:T(2,128)(2,1)}, u32[]{:S(2)}, u32[]{:S(2)}) async-start(bf16[64,2,3584]{2,1,0:T(2,128)(2,1)} %bitcast.64), calls=%async_computation | async-start | bytes 1835008 | tf_op jit(solution)/shard_map/all_to_all | solution.py:118
  125.9 2.4 copy-start.1
  172.6 58.4 %all-to-all-start.4 = ((bf16[64,2,3584]{2,1,0:T(2,128)(2,1)}), bf16[64,2,3584]{2,1,0:T(2,128)(2,1)}, u32[]{:S(2)}, u32[]{:S(2)}) async-start(bf16[64,2,3584]{2,1,0:T(2,128)(2,1)} %reshape.130), calls=%async_computation.4 | async-start | bytes 1835008 | tf_op jit(solution)/shard_map/all_to_all | solution.py:126
  231.0 58.4 %all-to-all-start.1 = ((bf16[64,2,3584]{2,1,0:T(2,128)(2,1)}), bf16[64,2,3584]{2,1,0:T(2,128)(2,1)}, u32[]{:S(2)}, u32[]{:S(2)}) async-start(bf16[64,2,3584]{2,1,0:T(2,128)(2,1)} %reshape.124), calls=%async_computation.1 | async-start | bytes 1835008 | tf_op jit(solution)/shard_map/all_to_all | solution.py:125
  240.2 67.0 %reduce-scatter.2.cloned.1.call-start = ((), (), s32[]{:S(2)}) async-start(), calls=%async_computation.6 | async-start | bytes 2293760 | tf_op jit(solution)/shard_map/reduce_scatter | solution.py:72
  292.3 6.5 %collective-permute-start = (bf16[1,8,3584]{2,1,0:T(8,128)(2,1)S(1)}, bf16[1,8,3584]{2,1,0:T(8,128)(2,1)S(1)}, u32[]{:S(2)}, u32[]{:S(2)}) collective-permute-start(bf16[1,8,3584]{2,1,0:T(8,128)(2,1)S(1)} %fusion.1), channel_id=1, source_target_pairs={{768,0},{0,256},{256,512},{512,768},{769,1},{1,257},{257,513},{513... | collective-permute-start | bytes 172040 | tf_op jit(solution)/shard_map/ppermute | solution.py:10
Sparse Core Ops, SparseCore 0:
  244.5 62.7 reduce-scatter.1
where the time goes:
time: 318 us; the launch traced here: 317 us
  waiting for transfers between devices  197 us (62%)
  starting transfers between devices  61.4 us (19%)
  local copies, waits for them, and re-layouts  19.4 us (6%)
  matrix products  15.8 us (5%)
  between operations  14.3 us (4%)
  other arithmetic  8.69 us (3%)
    all_to_all x1, waiting for transfers between devices, on_device(): lax.all_to_all(send_g, 'expert', split_axis=0, concat_axis=0, tiled=True)  48.3 us
    all_to_all x1, waiting for transfers between devices, on_device(): lax.all_to_all(out_rows, 'expert', split_axis=0, concat_axis=0, tiled=True)  44.6 us
    all_to_all x1, waiting for transfers between devices, on_device(): lax.all_to_all(send_x, 'expert', split_axis=0, concat_axis=0, tiled=True)  38.7 us
    all_to_all x1, waiting for transfers between devices, on_device(): lax.all_to_all(dx_rows, 'expert', split_axis=0, concat_axis=0, tiled=True)  36.8 us
    all_to_all x1, starting transfers between devices, on_device(): lax.all_to_all(pre_rows, 'expert', split_axis=0, concat_axis=0, tiled=True)  26.1 us
    all_to_all x1, waiting for transfers between devices, on_device(): lax.all_to_all(pre_rows, 'expert', split_axis=0, concat_axis=0, tiled=True)  18.1 us
    all_to_all x1, starting transfers between devices, on_device(): lax.all_to_all(dx_rows, 'expert', split_axis=0, concat_axis=0, tiled=True)  9.22 us
    all_to_all x1, starting transfers between devices, on_device(): lax.all_to_all(out_rows, 'expert', split_axis=0, concat_axis=0, tiled=True)  9.21 us
  transfers between devices with their start and end apart: 7, of which 7 were waited for; matrix products, arithmetic and copies ran while one was open for 11% of the time, Pallas kernels for 0%

commit v1 on v0

v1 whole, which is shorter than its diff:
```python
import functools

import jax
import jax.numpy as jnp
from jax import lax
from jax.experimental import pallas as pl
from jax.experimental.pallas import tpu as pltpu
from jax.sharding import PartitionSpec as P

EXPERTS = 16
SLOTS = 2
SHARDS = 4
ROWS = EXPERTS * SLOTS
BF = jnp.bfloat16
F32 = jnp.float32


def route_groups(replicas):
    groups = []
    for r in range(replicas):
        for shard in range(SHARDS):
            groups.append(
                [
                    (e * SHARDS + shard) * replicas
                    + (r if e < EXPERTS // 2 else replicas - 1 - r)
                    for e in range(EXPERTS)
                ]
            )
    return groups


def route(rows):
    groups = route_groups(lax.axis_size("dp"))
    return lax.all_to_all(
        rows,
        ("expert", "dp"),
        split_axis=0,
        concat_axis=0,
        tiled=True,
        axis_index_groups=groups,
    )


def swap(rows, bit):
    count = lax.axis_size("expert")
    return lax.ppermute(rows, "expert", [(i, i ^ bit) for i in range(count)])


def selections(ids_ref):
    tokens, chosen = ids_ref.shape
    lane = lax.broadcasted_iota(jnp.int32, (tokens, ROWS), 1)
    hits = [ids_ref[:, k : k + 1] == lane // SLOTS for k in range(chosen)]
    hit = jnp.where(functools.reduce(jnp.logical_or, hits), 1.0, 0.0)
    row = lax.broadcasted_iota(jnp.int32, (tokens, tokens), 0)
    col = lax.broadcasted_iota(jnp.int32, (tokens, tokens), 1)
    earlier = jnp.where(col < row, 1.0, 0.0)
    before = jnp.dot(earlier, hit, preferred_element_type=F32)
    slot = (lane % SLOTS).astype(F32)
    return [jnp.where(jnp.logical_and(h, before == slot), 1.0, 0.0) for h in hits]


def pick(sel, rows):
    return lax.dot_general(
        sel.astype(BF), rows, (((0,), (0,)), ((), ())), preferred_element_type=F32
    )


def build_kernel(
    shard_ref, ids_f, prob_f, x_ref, ids_b, prob_b, g_ref, pre_ref,
    sx_ref, sg_ref, wf_ref, tb_ref,
):
    sel_b = selections(ids_b)
    width = g_ref.shape[1]
    total = jnp.zeros((ROWS, width), F32)
    grad = g_ref[...].astype(F32)
    for k, sel in enumerate(sel_b):
        total += pick(sel, (prob_b[:, k : k + 1] * grad).astype(BF))
    sg_ref[:, :width] = total.astype(BF)
    chosen = len(sel_b)
    hid = pre_ref.shape[1] // (2 * chosen)
    units = hid // SHARDS
    shard = shard_ref[0]
    for step in range(SHARDS):
        for half in range(2):
            part = jnp.zeros((ROWS, units), F32)
            for k, sel in enumerate(sel_b):
                start = (2 * k + half) * hid + (shard ^ step) * units
                start = pl.multiple_of(start, 128)
                part += pick(sel, pre_ref[:, pl.ds(start, units)])
            at = width + (2 * step + half) * units
            sg_ref[:, at : at + units] = part.astype(BF)
    tb_ref[...] = sel_b[0] + sel_b[1]
    sel_f = selections(ids_f)
    sx_ref[...] = pick(sel_f[0] + sel_f[1], x_ref[...]).astype(BF)
    wf_ref[...] = sel_f[0] * prob_f[:, 0:1] + sel_f[1] * prob_f[:, 1:2]


def build_rows(shard, ids_f, prob_f, x, ids_b, prob_b, grad, pre):
    tokens, width = x.shape
    pre_width = pre.shape[1] // 2
    vmem = pl.BlockSpec(memory_space=pltpu.VMEM)
    return pl.pallas_call(
        build_kernel,
        out_shape=(
            jax.ShapeDtypeStruct((ROWS, width), BF),
            jax.ShapeDtypeStruct((ROWS, width + pre_width), BF),
            jax.ShapeDtypeStruct((tokens, ROWS), F32),
            jax.ShapeDtypeStruct((tokens, ROWS), F32),
        ),
        in_specs=[pl.BlockSpec(memory_space=pltpu.SMEM)] + [vmem] * 7,
        out_specs=(vmem,) * 4,
        cost_estimate=pl.CostEstimate(
            flops=4 * ROWS * tokens * width, bytes_accessed=2 << 20, transcendentals=0
        ),
        compiler_params=pltpu.CompilerParams(vmem_limit_bytes=16 << 20),
        name="build_rows",
    )(shard, ids_f, prob_f, x, ids_b, prob_b, grad, pre)


def silu_pair(value):
    sig = jax.nn.sigmoid(value)
    return (value * sig, sig * (1.0 + value * (1.0 - sig)))


CONTRACT = (((1,), (1,)), ((), ()))


def reduce_shards(partial):
    quarter = partial.shape[0] // SHARDS
    got = swap(partial[2 * quarter :].astype(BF), 1)
    pair = partial[: 2 * quarter] + got.astype(F32)
    got = swap(pair[quarter:].astype(BF), 2)
    return (pair[:quarter] + got.astype(F32)).astype(BF)


def routed_back(rows):
    width = rows.shape[1]
    back = route(rows.reshape(EXPERTS, SLOTS, width))
    return back.reshape(ROWS, width)


def combine(table, rows):
    return lax.dot_general(
        table,
        rows.astype(F32),
        (((1,), (0,)), ((), ())),
        precision=lax.Precision.HIGHEST,
        preferred_element_type=F32,
    ).astype(BF)


def on_device(x_fwd, ids_fwd, prob_fwd, grad_bwd, ids_bwd, prob_bwd, pre_bwd, w_gate, w_up, w_down):
    tokens, width = x_fwd.shape[1:]
    wg, wu, wd = w_gate[0], w_up[0], w_down[0]
    units = wg.shape[1]
    shard = (lax.axis_index("expert") % SHARDS).astype(jnp.int32).reshape(1)
    send_x, send_g, table_f, table_b = build_rows(
        shard, ids_fwd[0], prob_fwd[0], x_fwd[0], ids_bwd[0], prob_bwd[0], grad_bwd[0],
        pre_bwd[0].reshape(tokens, -1),
    )

    got_g = route(send_g.reshape(EXPERTS, SLOTS, -1)).reshape(ROWS, -1)
    got_x = route(send_x.reshape(EXPERTS, SLOTS, -1)).reshape(ROWS, -1)

    near, far = width + 2 * units, width + 4 * units
    other = swap(jnp.concatenate([got_g[:, :width], got_g[:, far:]], axis=1), 2)
    mine = jnp.concatenate([got_g[:, :far], other], axis=0)
    beside = swap(jnp.concatenate([mine[:, :width], mine[:, near:]], axis=1), 1)
    rows = jnp.concatenate([mine[:, :near], beside], axis=0)
    flat_g = rows[:, :width]
    pre = rows[:, width:].astype(F32)
    gate_pre, up_pre = pre[:, :units], pre[:, units:]
    act, slope = silu_pair(gate_pre)
    hidden = (act * up_pre).astype(BF)
    grad_rows = lax.psum_scatter(
        lax.dot_general(
            hidden, flat_g, (((0,), (0,)), ((), ())), preferred_element_type=F32
        ).astype(BF),
        "dp",
        scatter_dimension=0,
        tiled=True,
    ).astype(F32)
    dhid = lax.dot_general(flat_g, wd, CONTRACT, preferred_element_type=F32)
    d_gate = (dhid * up_pre * slope).astype(BF)
    d_up = (dhid * act).astype(BF)
    dx_part = lax.dot_general(d_gate, wg, CONTRACT, preferred_element_type=F32)
    dx_part = dx_part + lax.dot_general(d_up, wu, CONTRACT, preferred_element_type=F32)
    back_dx = routed_back(reduce_shards(dx_part))

    mine = jnp.concatenate([got_x, swap(got_x, 2)], axis=0)
    rows = jnp.concatenate([mine, swap(mine, 1)], axis=0)
    act, _ = silu_pair(jnp.dot(rows, wg, preferred_element_type=F32))
    up = jnp.dot(rows, wu, preferred_element_type=F32)
    y_part = jnp.dot((act * up).astype(BF), wd, preferred_element_type=F32)
    back_y = routed_back(reduce_shards(y_part))

    routed = combine(table_f, back_y)
    sections = lax.axis_size("pipe")
    moved = lax.ppermute(routed, "pipe", [(i, (i + 1) % sections) for i in range(sections)])
    grad_input = combine(table_b, back_dx)
    return (moved[None], grad_input[None], grad_rows[None])


def solution(mesh):
    token = P("pipe", ("expert", "dp"), None)
    in_specs = (
        token, token, token, token, token, token,
        P("pipe", ("expert", "dp"), None, None, None),
        P("pipe", None, "expert"),
        P("pipe", None, "expert"),
        P("pipe", "expert", None),
    )
    return jax.shard_map(
        on_device, mesh=mesh, in_specs=in_specs, out_specs=(token, token, token), check_vma=False
    )
```

time: 318 us -> 203 us (0.64)
  the two profiles are of different devices: /device:TPU:1 before, /device:TPU:140 now
where the time goes in v1:
time: 203 us; the launch traced here: 202 us
  waiting for transfers between devices  79.6 us (39%)
  starting transfers between devices  71.7 us (35%)
  local copies, waits for them, and re-layouts  16.4 us (8%)
  between operations  14.4 us (7%)
  matrix products  11.5 us (6%)
  other arithmetic  7.18 us (4%)
    all_to_all x4, waiting for transfers between devices, route(): lax.all_to_all(rows, ('expert', 'dp'), split_axis=0, concat_axis=0, tiled...  50.1 us
    all_to_all x4, starting transfers between devices, route(): lax.all_to_all(rows, ('expert', 'dp'), split_axis=0, concat_axis=0, tiled...  48.6 us
    ppermute x8, waiting for transfers between devices, swap(): return lax.ppermute(rows, 'expert', [(i, i ^ bit) for i in range(count)])  26.5 us
    ppermute x8, starting transfers between devices, swap(): return lax.ppermute(rows, 'expert', [(i, i ^ bit) for i in range(count)])  19.9 us
  transfers between devices with their start and end apart: 14, of which 6 were waited for; matrix products, arithmetic and copies ran while one was open for 12% of the time, Pallas kernels for 0%

profile of v1, /device:TPU:140, one launch (start us, length us, event | category | flops | bytes accessed | tf_op | source)
XLA Modules:
  0.0 201.6 jit_solution(4260079151499936026)
XLA Ops:
  7.2 0.0 copy-start
  7.2 1.0 reshape_squeeze.3.pre_ref
  8.2 0.8 copy.13.ids_f
  9.0 0.8 copy.14.prob_f
  9.7 0.8 copy.15.ids_b
  10.5 0.8 copy.16.prob_b
  11.2 0.8 copy-done.1
  12.0 0.8 copy-done.2
  12.9 0.8 build_rows.1
  13.7 0.8 reshape.34
  14.4 21.1 %all-to-all-start = ((bf16[16,2,3584]{2,1,0:T(2,128)(2,1)}), bf16[16,2,3584]{2,1,0:T(2,128)(2,1)S(1)}, u32[]{:S(2)}, u32[]{:S(2)}) async-start(bf16[16,2,3584]{2,1,0:T(2,128)(2,1)} %reshape.34), calls=%async_computation | async-start | bytes 458752 | tf_op jit(solution)/shard_map/all_to_all | solution.py:34
  35.5 0.9 reshape.38
  36.4 17.3 %all-to-all-done = bf16[16,2,3584]{2,1,0:T(2,128)(2,1)S(1)} async-done(((bf16[16,2,3584]{2,1,0:T(2,128)(2,1)}), bf16[16,2,3584]{2,1,0:T(2,128)(2,1)S(1)}, u32[]{:S(2)}, u32[]{:S(2)}) %all-to-all-start) | async-done | bytes 229408 | tf_op jit(solution)/shard_map/all_to_all | solution.py:34
  53.7 8.2 %all-to-all-start.2 = ((bf16[16,2,5632]{2,1,0:T(2,128)(2,1)}), bf16[16,2,5632]{2,1,0:T(2,128)(2,1)S(1)}, u32[]{:S(2)}, u32[]{:S(2)}) async-start(bf16[16,2,5632]{2,1,0:T(2,128)(2,1)} %reshape.38), calls=%async_computation.2 | async-start | bytes 720896 | tf_op jit(solution)/shard_map/all_to_all | solution.py:34
  61.9 0.0 reduce-scatter.2.cloned.1.call-start
  62.0 0.1 reshape.35
  62.1 3.6 %collective-permute-start = (bf16[32,3584]{1,0:T(8,128)(2,1)S(1)}, bf16[32,3584]{1,0:T(8,128)(2,1)S(1)}, u32[]{:S(2)}, u32[]{:S(2)}) collective-permute-start(bf16[32,3584]{1,0:T(8,128)(2,1)S(1)} %reshape.35), channel_id=1, source_target_pairs={{0,8},{4,12},{8,0},{12,4},{16,24},{20,28},{24,16},{28,20},{32,40},... | collective-permute-start | bytes 688136 | tf_op jit(solution)/shard_map/ppermute | solution.py:46
  65.7 18.5 %collective-permute-done = bf16[32,3584]{1,0:T(8,128)(2,1)S(1)} collective-permute-done((bf16[32,3584]{1,0:T(8,128)(2,1)S(1)}, bf16[32,3584]{1,0:T(8,128)(2,1)S(1)}, u32[]{:S(2)}, u32[]{:S(2)}) %collective-permute-start) | collective-permute-done | bytes 229408 | tf_op jit(solution)/shard_map/ppermute | solution.py:46
  84.2 0.8 pad_maximum_fusion
  85.0 1.9 collective-permute-start.1
  86.9 0.1 reshape.39
  87.2 0.0 copy-start.3
  87.2 2.3 %collective-permute-start.5 = (bf16[32,4608]{1,0:T(8,128)(2,1)S(1)}, bf16[32,4608]{1,0:T(8,128)(2,1)S(1)}, u32[]{:S(2)}, u32[]{:S(2)}) collective-permute-start(bf16[32,4608]{1,0:T(8,128)(2,1)S(1)} %pad_maximum_fusion.1), channel_id=1, source_target_pairs={{0,8},{4,12},{8,0},{12,4},{16,24},{20,28},{24,16},{28,20},{32,40},... | collective-permute-start | bytes 884744 | tf_op jit(solution)/shard_map/ppermute | solution.py:46
  89.6 1.1 constant_dynamic-update-slice_fusion
  90.6 8.0 %collective-permute-done.5 = bf16[32,4608]{1,0:T(8,128)(2,1)S(1)} collective-permute-done((bf16[32,4608]{1,0:T(8,128)(2,1)S(1)}, bf16[32,4608]{1,0:T(8,128)(2,1)S(1)}, u32[]{:S(2)}, u32[]{:S(2)}) %collective-permute-start.5) | collective-permute-done | bytes 294944 | tf_op jit(solution)/shard_map/ppermute | solution.py:46
  98.7 0.9 fusion.17
  99.6 1.9 collective-permute-start.6
  101.5 0.4 fusion.6
  101.9 4.0 %fusion.3 = f32[128,3584]{1,0:T(8,128)} fusion(bf16[1,256,3584]{2,1,0:T(8,128)(2,1)} %param.19, f32[128,256]{1,0:T(8,128)S(1)} %fusion.6, bf16[128,3584]{1,0:T(8,128)(2,1)S(1)} %constant_dynamic-update-slice_fusion, bf16[1,3584,256]{2,1,0:T(8,128)(2,1)S(1)} %copy-done), kind=kOutput, calls=%fused_computation.7 | convolution fusion | flops 469958656 | bytes 6553600 | tf_op jit(solution)/shard_map/dot_general | solution.py:194
  105.9 1.4 slice.143
  107.2 2.4 %collective-permute-start.2 = (bf16[64,3584]{1,0:T(8,128)(2,1)S(1)}, bf16[64,3584]{1,0:T(8,128)(2,1)S(1)}, u32[]{:S(2)}, u32[]{:S(2)}) collective-permute-start(bf16[64,3584]{1,0:T(8,128)(2,1)S(1)} %slice.143), channel_id=1, source_target_pairs={{0,4},{4,0},{8,12},{12,8},{16,20},{20,16},{24,28},{28,24},{32,36},... | collective-permute-start | bytes 1376264 | tf_op jit(solution)/shard_map/ppermute | solution.py:46
  109.7 0.9 fusion.21
  110.6 1.7 fusion.1
  112.3 0.0 copy-start.4
  112.3 0.7 fusion.8
  113.0 0.8 copy-done.4
  113.8 0.7 convolution_add_fusion
  114.5 0.9 slice.142
  115.4 1.9 collective-permute-start.7
  117.3 0.1 slice_add_fusion.1
  117.4 0.7 slice.145
  118.2 2.2 %collective-permute-start.3 = (bf16[32,3584]{1,0:T(8,128)(2,1)}, bf16[32,3584]{1,0:T(8,128)(2,1)S(1)}, u32[]{:S(2)}, u32[]{:S(2)}) collective-permute-start(bf16[32,3584]{1,0:T(8,128)(2,1)} %slice.145), channel_id=1, source_target_pairs={{0,8},{4,12},{8,0},{12,4},{16,24},{20,28},{24,16},{28,20},{32,40},... | collective-permute-start | bytes 688136 | tf_op jit(solution)/shard_map/ppermute | solution.py:46
  120.4 3.0 %convolution_convert_fusion = bf16[256,3584]{1,0:T(8,128)(2,1)} fusion(f32[128,512]{1,0:T(8,128)S(1)} %fusion.21, bf16[64,4096]{1,0:T(8,128)(2,1)S(1)} %get-tuple-element.12, bf16[64,4096]{1,0:T(8,128)(2,1)} %collective-permute-done.6), kind=kOutput, calls=%fused_computation | convolution fusion | flops 237830144 | bytes 3145728 | tf_op jit(solution)/shard_map/dot_general | solution.py:176
  123.3 0.0 reduce-scatter.2.cloned.1.call-update
  123.3 1.4 slice_add_fusion
  124.7 0.0 copy-start.7
  124.7 0.9 copy-done.7
  125.7 0.7 slice.144
  126.4 3.6 %collective-permute-start.8 = (bf16[32,3584]{1,0:T(8,128)(2,1)}, bf16[32,3584]{1,0:T(8,128)(2,1)S(1)}, u32[]{:S(2)}, u32[]{:S(2)}) collective-permute-start(bf16[32,3584]{1,0:T(8,128)(2,1)} %slice.144), channel_id=1, source_target_pairs={{0,8},{4,12},{8,0},{12,4},{16,24},{20,28},{24,16},{28,20},{32,40},... | collective-permute-start | bytes 688136 | tf_op jit(solution)/shard_map/ppermute | solution.py:46
  130.1 0.8 reshape.36
  130.8 13.4 %all-to-all-start.1 = ((bf16[16,2,3584]{2,1,0:T(2,128)(2,1)}), bf16[16,2,3584]{2,1,0:T(2,128)(2,1)S(1)}, u32[]{:S(2)}, u32[]{:S(2)}) async-start(bf16[16,2,3584]{2,1,0:T(2,128)(2,1)} %reshape.36), calls=%async_computation.1 | async-start | bytes 458752 | tf_op jit(solution)/shard_map/all_to_all | solution.py:34
  144.2 1.1 fusion.19
  145.3 0.8 reshape.40
  146.1 19.0 %all-to-all-done.1 = bf16[16,2,3584]{2,1,0:T(2,128)(2,1)S(1)} async-done(((bf16[16,2,3584]{2,1,0:T(2,128)(2,1)}), bf16[16,2,3584]{2,1,0:T(2,128)(2,1)S(1)}, u32[]{:S(2)}, u32[]{:S(2)}) %all-to-all-start.1) | async-done | bytes 229408 | tf_op jit(solution)/shard_map/all_to_all | solution.py:34
  165.0 5.9 %all-to-all-start.3 = ((bf16[16,2,3584]{2,1,0:T(2,128)(2,1)}), bf16[16,2,3584]{2,1,0:T(2,128)(2,1)S(1)}, u32[]{:S(2)}, u32[]{:S(2)}) async-start(bf16[16,2,3584]{2,1,0:T(2,128)(2,1)} %reshape.40), calls=%async_computation.3 | async-start | bytes 458752 | tf_op jit(solution)/shard_map/all_to_all | solution.py:34
  170.9 0.1 reshape.37
  171.0 0.2 convolution_convert_fusion.2
  171.2 3.1 %collective-permute-start.4 = (bf16[8,3584]{1,0:T(8,128)(2,1)S(1)}, bf16[8,3584]{1,0:T(8,128)(2,1)S(1)}, u32[]{:S(2)}, u32[]{:S(2)}) collective-permute-start(bf16[8,3584]{1,0:T(8,128)(2,1)S(1)} %convolution_convert_fusion.2), channel_id=1, source_target_pairs={{0,256},{256,512},{512,768},{768,0},{1,257},{257,513},{513,769},{7... | collective-permute-start | bytes 172040 | tf_op jit(solution)/shard_map/ppermute | solution.py:199
  174.4 2.9 %collective-permute-done.4 = bf16[8,3584]{1,0:T(8,128)(2,1)S(1)} collective-permute-done((bf16[8,3584]{1,0:T(8,128)(2,1)S(1)}, bf16[8,3584]{1,0:T(8,128)(2,1)S(1)}, u32[]{:S(2)}, u32[]{:S(2)}) %collective-permute-start.4) | collective-permute-done | bytes 57376 | tf_op jit(solution)/shard_map/ppermute | solution.py:199
  177.3 13.9 %all-to-all-done.3 = bf16[16,2,3584]{2,1,0:T(2,128)(2,1)S(1)} async-done(((bf16[16,2,3584]{2,1,0:T(2,128)(2,1)}), bf16[16,2,3584]{2,1,0:T(2,128)(2,1)S(1)}, u32[]{:S(2)}, u32[]{:S(2)}) %all-to-all-start.3) | async-done | bytes 229408 | tf_op jit(solution)/shard_map/all_to_all | solution.py:34
  191.2 0.1 reshape.41
  191.2 0.8 fusion
  192.1 2.0 bitcast_convert_fusion
  194.1 0.6 copy.20
  (26 shorter events, 0.2 us)
Async XLA Ops:
  7.2 94.8 %copy-start = (bf16[1,3584,256]{2,1,0:T(8,128)(2,1)S(1)}, bf16[1,3584,256]{2,1,0:T(8,128)(2,1)}, u32[]{:S(2)}) copy-start(bf16[1,3584,256]{2,1,0:T(8,128)(2,1)} %param.17) | copy-start | bytes 5505028
  11.2 0.8 copy-start.1
  12.0 0.8 copy-start.2
  14.4 39.3 %all-to-all-start = ((bf16[16,2,3584]{2,1,0:T(2,128)(2,1)}), bf16[16,2,3584]{2,1,0:T(2,128)(2,1)S(1)}, u32[]{:S(2)}, u32[]{:S(2)}) async-start(bf16[16,2,3584]{2,1,0:T(2,128)(2,1)} %reshape.34), calls=%async_computation | async-start | bytes 458752 | tf_op jit(solution)/shard_map/all_to_all | solution.py:34
  53.7 33.2 %all-to-all-start.2 = ((bf16[16,2,5632]{2,1,0:T(2,128)(2,1)}), bf16[16,2,5632]{2,1,0:T(2,128)(2,1)S(1)}, u32[]{:S(2)}, u32[]{:S(2)}) async-start(bf16[16,2,5632]{2,1,0:T(2,128)(2,1)} %reshape.38), calls=%async_computation.2 | async-start | bytes 720896 | tf_op jit(solution)/shard_map/all_to_all | solution.py:34
  61.9 130.2 %reduce-scatter.2.cloned.1.call-start = ((), (), s32[]{:S(2)}) async-start(), calls=%async_computation.5 | async-start | bytes 2293760 | tf_op jit(solution)/shard_map/reduce_scatter | solution.py:175
  62.1 22.1 %collective-permute-start = (bf16[32,3584]{1,0:T(8,128)(2,1)S(1)}, bf16[32,3584]{1,0:T(8,128)(2,1)S(1)}, u32[]{:S(2)}, u32[]{:S(2)}) collective-permute-start(bf16[32,3584]{1,0:T(8,128)(2,1)S(1)} %reshape.35), channel_id=1, source_target_pairs={{0,8},{4,12},{8,0},{12,4},{16,24},{20,28},{24,16},{28,20},{32,40},... | collective-permute-start | bytes 688136 | tf_op jit(solution)/shard_map/ppermute | solution.py:46
  85.0 4.6 %collective-permute-start.1 = (bf16[64,3584]{1,0:T(8,128)(2,1)}, bf16[64,3584]{1,0:T(8,128)(2,1)}, u32[]{:S(2)}, u32[]{:S(2)}) collective-permute-start(bf16[64,3584]{1,0:T(8,128)(2,1)} %pad_maximum_fusion), channel_id=1, source_target_pairs={{0,4},{4,0},{8,12},{12,8},{16,20},{20,16},{24,28},{28,24},{32,36},... | collective-permute-start | bytes 1376264 | tf_op jit(solution)/shard_map/ppermute | solution.py:46
  87.2 14.3 %copy-start.3 = (bf16[1,3584,256]{2,1,0:T(8,128)(2,1)S(1)}, bf16[1,3584,256]{2,1,0:T(8,128)(2,1)}, u32[]{:S(2)}) copy-start(bf16[1,3584,256]{2,1,0:T(8,128)(2,1)} %param.18) | copy-start | bytes 5505028
  87.2 11.4 %collective-permute-start.5 = (bf16[32,4608]{1,0:T(8,128)(2,1)S(1)}, bf16[32,4608]{1,0:T(8,128)(2,1)S(1)}, u32[]{:S(2)}, u32[]{:S(2)}) collective-permute-start(bf16[32,4608]{1,0:T(8,128)(2,1)S(1)} %pad_maximum_fusion.1), channel_id=1, source_target_pairs={{0,8},{4,12},{8,0},{12,4},{16,24},{20,28},{24,16},{28,20},{32,40},... | collective-permute-start | bytes 884744 | tf_op jit(solution)/shard_map/ppermute | solution.py:46
  99.6 10.1 %collective-permute-start.6 = (bf16[64,4096]{1,0:T(8,128)(2,1)}, bf16[64,4096]{1,0:T(8,128)(2,1)}, u32[]{:S(2)}, u32[]{:S(2)}) collective-permute-start(bf16[64,4096]{1,0:T(8,128)(2,1)} %get-tuple-element.11), channel_id=1, source_target_pairs={{0,4},{4,0},{8,12},{12,8},{16,20},{20,16},{24,28},{28,24},{32,36},... | collective-permute-start | bytes 1572872 | tf_op jit(solution)/shard_map/ppermute | solution.py:46
  105.9 4.7 %copy-start.8 = (bf16[1,256,3584]{2,1,0:T(8,128)(2,1)S(1)}, bf16[1,256,3584]{2,1,0:T(8,128)(2,1)}, u32[]{:S(2)}) copy-start(bf16[1,256,3584]{2,1,0:T(8,128)(2,1)} %param.19) | copy-start | bytes 5505028
  107.2 10.1 %collective-permute-start.2 = (bf16[64,3584]{1,0:T(8,128)(2,1)S(1)}, bf16[64,3584]{1,0:T(8,128)(2,1)S(1)}, u32[]{:S(2)}, u32[]{:S(2)}) collective-permute-start(bf16[64,3584]{1,0:T(8,128)(2,1)S(1)} %slice.143), channel_id=1, source_target_pairs={{0,4},{4,0},{8,12},{12,8},{16,20},{20,16},{24,28},{28,24},{32,36},... | collective-permute-start | bytes 1376264 | tf_op jit(solution)/shard_map/ppermute | solution.py:46
  112.3 1.5 copy-start.4
  113.8 3.5 %copy-start.6 = (f32[128,3584]{1,0:T(8,128)S(1)}, f32[128,3584]{1,0:T(8,128)}, u32[]{:S(2)}) copy-start(f32[128,3584]{1,0:T(8,128)} %fusion.3) | copy-start | bytes 5505028
  114.5 3.6 %copy-start.5 = (f32[128,3584]{1,0:T(8,128)}, f32[128,3584]{1,0:T(8,128)S(1)}, u32[]{:S(2)}) copy-start(f32[128,3584]{1,0:T(8,128)S(1)} %convolution_add_fusion) | copy-start | bytes 5505028
  115.4 7.9 %collective-permute-start.7 = (bf16[64,3584]{1,0:T(8,128)(2,1)}, bf16[64,3584]{1,0:T(8,128)(2,1)}, u32[]{:S(2)}, u32[]{:S(2)}) collective-permute-start(bf16[64,3584]{1,0:T(8,128)(2,1)} %slice.142), channel_id=1, source_target_pairs={{0,4},{4,0},{8,12},{12,8},{16,20},{20,16},{24,28},{28,24},{32,36},... | collective-permute-start | bytes 1376264 | tf_op jit(solution)/shard_map/ppermute | solution.py:46
  118.2 11.9 %collective-permute-start.3 = (bf16[32,3584]{1,0:T(8,128)(2,1)}, bf16[32,3584]{1,0:T(8,128)(2,1)S(1)}, u32[]{:S(2)}, u32[]{:S(2)}) collective-permute-start(bf16[32,3584]{1,0:T(8,128)(2,1)} %slice.145), channel_id=1, source_target_pairs={{0,8},{4,12},{8,0},{12,4},{16,24},{20,28},{24,16},{28,20},{32,40},... | collective-permute-start | bytes 688136 | tf_op jit(solution)/shard_map/ppermute | solution.py:46
  124.7 0.9 copy-start.7
  126.4 17.8 %collective-permute-start.8 = (bf16[32,3584]{1,0:T(8,128)(2,1)}, bf16[32,3584]{1,0:T(8,128)(2,1)S(1)}, u32[]{:S(2)}, u32[]{:S(2)}) collective-permute-start(bf16[32,3584]{1,0:T(8,128)(2,1)} %slice.144), channel_id=1, source_target_pairs={{0,8},{4,12},{8,0},{12,4},{16,24},{20,28},{24,16},{28,20},{32,40},... | collective-permute-start | bytes 688136 | tf_op jit(solution)/shard_map/ppermute | solution.py:46
  130.8 34.2 %all-to-all-start.1 = ((bf16[16,2,3584]{2,1,0:T(2,128)(2,1)}), bf16[16,2,3584]{2,1,0:T(2,128)(2,1)S(1)}, u32[]{:S(2)}, u32[]{:S(2)}) async-start(bf16[16,2,3584]{2,1,0:T(2,128)(2,1)} %reshape.36), calls=%async_computation.1 | async-start | bytes 458752 | tf_op jit(solution)/shard_map/all_to_all | solution.py:34
  165.0 26.1 %all-to-all-start.3 = ((bf16[16,2,3584]{2,1,0:T(2,128)(2,1)}), bf16[16,2,3584]{2,1,0:T(2,128)(2,1)S(1)}, u32[]{:S(2)}, u32[]{:S(2)}) async-start(bf16[16,2,3584]{2,1,0:T(2,128)(2,1)} %reshape.40), calls=%async_computation.3 | async-start | bytes 458752 | tf_op jit(solution)/shard_map/all_to_all | solution.py:34
  171.2 6.1 %collective-permute-start.4 = (bf16[8,3584]{1,0:T(8,128)(2,1)S(1)}, bf16[8,3584]{1,0:T(8,128)(2,1)S(1)}, u32[]{:S(2)}, u32[]{:S(2)}) collective-permute-start(bf16[8,3584]{1,0:T(8,128)(2,1)S(1)} %convolution_convert_fusion.2), channel_id=1, source_target_pairs={{0,256},{256,512},{512,768},{768,0},{1,257},{257,513},{513,769},{7... | collective-permute-start | bytes 172040 | tf_op jit(solution)/shard_map/ppermute | solution.py:199
Sparse Core Ops, SparseCore 0:
  123.5 50.6 reduce-scatter.1

commit v2 on v1

v2 whole, which is shorter than its diff:
```python
import functools

import jax
import jax.numpy as jnp
from jax import lax
from jax.experimental import pallas as pl
from jax.experimental.pallas import tpu as pltpu
from jax.sharding import PartitionSpec as P

EXPERTS = 16
SLOTS = 2
SHARDS = 4
ROWS = EXPERTS * SLOTS
BF = jnp.bfloat16
F32 = jnp.float32


def route_groups(replicas):
    groups = []
    for r in range(replicas):
        for shard in range(SHARDS):
            groups.append(
                [
                    (e * SHARDS + (shard ^ 2 * far_half(e))) * replicas
                    + (r if e < EXPERTS // 2 else replicas - 1 - r)
                    for e in range(EXPERTS)
                ]
            )
    return groups


def far_half(expert):
    ring = EXPERTS // 2
    return expert % ring // (ring // 2)


def route(rows):
    groups = route_groups(lax.axis_size("dp"))
    return lax.all_to_all(
        rows,
        ("expert", "dp"),
        split_axis=0,
        concat_axis=0,
        tiled=True,
        axis_index_groups=groups,
    )


def swap(rows, bit):
    count = lax.axis_size("expert")
    return lax.ppermute(rows, "expert", [(i, i ^ bit) for i in range(count)])


def selections(ids_ref):
    chosen, tokens = ids_ref.shape
    row = lax.broadcasted_iota(jnp.int32, (ROWS, tokens), 0)
    hits = [ids_ref[k : k + 1, :] == row // SLOTS for k in range(chosen)]
    hit = jnp.where(functools.reduce(jnp.logical_or, hits), 1.0, 0.0)
    first = lax.broadcasted_iota(jnp.int32, (tokens, tokens), 0)
    second = lax.broadcasted_iota(jnp.int32, (tokens, tokens), 1)
    earlier = jnp.where(first < second, 1.0, 0.0)
    before = jnp.dot(hit, earlier, preferred_element_type=F32)
    slot = (row % SLOTS).astype(F32)
    return [jnp.where(jnp.logical_and(h, before == slot), 1.0, 0.0) for h in hits]


def pick(sel, rows):
    return jnp.dot(sel.astype(BF), rows, preferred_element_type=F32)


def build_kernel(shard_ref, *refs):
    hbm, (send_ref, wf_ref, tb_ref), held, sem = refs[:7], refs[7:10], refs[10:17], refs[17]
    copies = [
        pltpu.make_async_copy(src, dst, sem.at[i]) for i, (src, dst) in enumerate(zip(hbm, held))
    ]
    for copy in copies:
        copy.start()
    for copy in copies:
        copy.wait()
    ids_f, prob_f, x_ref, ids_b, prob_b, g_ref, pre_ref = held
    width = g_ref.shape[1]
    sel_b = selections(ids_b)
    both = functools.reduce(jnp.add, sel_b)
    scaled = functools.reduce(jnp.add, [s * prob_b[k : k + 1, :] for k, s in enumerate(sel_b)])
    scale = jnp.sum(scaled, axis=1, keepdims=True)
    send_ref[:, :width] = (scale * pick(both, g_ref[...])).astype(BF)
    chosen = len(sel_b)
    hid = pre_ref.shape[1] // (2 * chosen)
    units = hid // SHARDS
    shard = shard_ref[0]
    blocks = []
    for step in range(SHARDS):
        halves = []
        for half in range(2):
            part = jnp.zeros((ROWS, units), F32)
            for k, sel in enumerate(sel_b):
                start = (2 * k + half) * hid + (shard ^ step) * units
                start = pl.multiple_of(start, 128)
                part += pick(sel, pre_ref[:, pl.ds(start, units)])
            halves.append(part)
        blocks.append(halves)
    expert = lax.broadcasted_iota(jnp.int32, (ROWS, units), 0) // SLOTS
    crosses = far_half(expert) != shard_ref[1]
    for step in range(SHARDS):
        for half in range(2):
            at = width + (2 * step + half) * units
            part = jnp.where(crosses, blocks[step ^ 2][half], blocks[step][half])
            send_ref[:, at : at + units] = part.astype(BF)
    tb_ref[...] = both
    sel_f = selections(ids_f)
    send_ref[:, width + 2 * hid :] = pick(functools.reduce(jnp.add, sel_f), x_ref[...]).astype(BF)
    wf_ref[...] = functools.reduce(
        jnp.add, [s * prob_f[k : k + 1, :] for k, s in enumerate(sel_f)]
    )


VMEM = pl.BlockSpec(memory_space=pltpu.VMEM)


def build_rows(place, *arrays):
    x, pre = arrays[2], arrays[6]
    tokens, width = x.shape
    total = 2 * width + pre.shape[1] // 2
    return pl.pallas_call(
        build_kernel,
        out_shape=(
            jax.ShapeDtypeStruct((ROWS, total), BF),
            jax.ShapeDtypeStruct((ROWS, tokens), F32),
            jax.ShapeDtypeStruct((ROWS, tokens), F32),
        ),
        in_specs=[pl.BlockSpec(memory_space=pltpu.SMEM)]
        + [pl.BlockSpec(memory_space=pl.ANY)] * len(arrays),
        out_specs=(VMEM,) * 3,
        scratch_shapes=[pltpu.VMEM(a.shape, a.dtype) for a in arrays]
        + [pltpu.SemaphoreType.DMA((len(arrays),))],
        cost_estimate=pl.CostEstimate(
            flops=4 * ROWS * tokens * width, bytes_accessed=2 << 20, transcendentals=0
        ),
        compiler_params=pltpu.CompilerParams(vmem_limit_bytes=48 << 20),
        name="build_rows",
    )(place, *arrays)


def silu_pair(value):
    sig = jax.nn.sigmoid(value)
    return (value * sig, sig * (1.0 + value * (1.0 - sig)))


CONTRACT = (((1,), (1,)), ((), ()))
CHUNK = 512


def call(kernel, outs, flops, *arrays):
    moved = sum(a.size * a.dtype.itemsize for a in arrays)
    moved += sum(o.size * o.dtype.itemsize for o in outs)
    return pl.pallas_call(
        kernel,
        out_shape=tuple(outs),
        in_specs=[VMEM] * len(arrays),
        out_specs=(VMEM,) * len(outs),
        cost_estimate=pl.CostEstimate(flops=flops, bytes_accessed=moved, transcendentals=0),
        compiler_params=pltpu.CompilerParams(vmem_limit_bytes=24 << 20),
        name=kernel.__name__,
    )(*arrays)


def store_halves(keep_ref, send_ref, cols, value):
    half = keep_ref.shape[0]
    keep_ref[:, cols] = value[:half]
    send_ref[:, cols] = value[half:].astype(BF)


def forward_kernel(own, near, beside, wg, wu, wd, keep_ref, send_ref):
    rows = jnp.concatenate([own[...], near[...], beside[...]], axis=0)
    act, _ = silu_pair(jnp.dot(rows, wg[...], preferred_element_type=F32))
    hidden = (act * jnp.dot(rows, wu[...], preferred_element_type=F32)).astype(BF)
    for at in range(0, wd.shape[1], CHUNK):
        cols = slice(at, at + CHUNK)
        value = jnp.dot(hidden, wd[:, cols], preferred_element_type=F32)
        store_halves(keep_ref, send_ref, cols, value)


def saved(own, near, beside, width, units):
    pre = jnp.concatenate(
        [ref[:, width : width + 2 * units] for ref in (own, near, beside)], axis=0
    ).astype(F32)
    return pre[:, :units], pre[:, units:]


def grad_kernel(own, near, beside, out_ref):
    units, width = out_ref.shape
    gate, up = saved(own, near, beside, width, units)
    act, _ = silu_pair(gate)
    hidden = (act * up).astype(BF).T
    for at in range(0, width, CHUNK):
        cols = slice(at, at + CHUNK)
        rows = jnp.concatenate([own[:, cols], near[:, cols], beside[:, cols]], axis=0)
        out_ref[:, cols] = jnp.dot(hidden, rows, preferred_element_type=F32).astype(BF)


def backward_kernel(own, near, beside, wg, wu, wd, keep_ref, send_ref):
    units, width = wd.shape
    gate, up = saved(own, near, beside, width, units)
    act, slope = silu_pair(gate)
    rows = jnp.concatenate([own[:, :width], near[:, :width], beside[:, :width]], axis=0)
    dhid = lax.dot_general(rows, wd[...], CONTRACT, preferred_element_type=F32)
    d_gate = (dhid * up * slope).astype(BF)
    d_up = (dhid * act).astype(BF)
    for at in range(0, width, CHUNK):
        cols = slice(at, at + CHUNK)
        value = lax.dot_general(d_gate, wg[cols, :], CONTRACT, preferred_element_type=F32)
        value += lax.dot_general(d_up, wu[cols, :], CONTRACT, preferred_element_type=F32)
        store_halves(keep_ref, send_ref, cols, value)


def pair_kernel(keep_ref, got_ref, own_ref, send_ref):
    half = own_ref.shape[0]
    for at in range(0, keep_ref.shape[1], CHUNK):
        cols = slice(at, at + CHUNK)
        store_halves(own_ref, send_ref, cols, keep_ref[:, cols] + got_ref[:, cols].astype(F32))


def halves_of(rows, width):
    half = rows // 2
    return [jax.ShapeDtypeStruct((half, width), F32), jax.ShapeDtypeStruct((half, width), BF)]


def reduce_shards(keep, send):
    rows, width = keep.shape
    own, send = call(pair_kernel, halves_of(rows, width), rows * width, keep, swap(send, 1))
    return (own + swap(send, 2).astype(F32)).astype(BF)


def combine(table, rows):
    return lax.dot_general(
        table,
        rows.astype(F32),
        (((0,), (0,)), ((), ())),
        precision=lax.Precision.HIGHEST,
        preferred_element_type=F32,
    ).astype(BF)


def on_device(x_fwd, ids_fwd, prob_fwd, grad_bwd, ids_bwd, prob_bwd, pre_bwd, w_gate, w_up, w_down):
    tokens, width = x_fwd.shape[1:]
    wg, wu, wd = w_gate[0], w_up[0], w_down[0]
    units = wg.shape[1]
    index = lax.axis_index("expert")
    place = jnp.stack([index % SHARDS, far_half(index // SHARDS)]).astype(jnp.int32)
    send, table_f, table_b = build_rows(
        place, ids_fwd[0].T, prob_fwd[0].T, x_fwd[0], ids_bwd[0].T, prob_bwd[0].T, grad_bwd[0],
        pre_bwd[0].reshape(tokens, -1),
    )
    sections = lax.axis_size("pipe")
    onward = [(i, (i + 1) % sections) for i in range(sections)]
    table_f = lax.ppermute(table_f, "pipe", onward)

    got = route(send.reshape(EXPERTS, SLOTS, -1)).reshape(ROWS, -1)
    pair, near, far, end = width + 2 * units, width + 4 * units, width + 6 * units, width + 8 * units
    other_g = swap(jnp.concatenate([got[:, :width], got[:, near:end]], axis=1), 2)
    got_x = got[:, end:]
    other_x = swap(got_x, 2)

    own_g = got[:, :near]
    mine = jnp.concatenate([own_g, other_g], axis=0)
    beside = swap(jnp.concatenate([mine[:, :width], mine[:, pair:]], axis=1), 1)
    work = 2 * SHARDS * ROWS * width * units
    (partial,) = call(
        grad_kernel, [jax.ShapeDtypeStruct(wd.shape, BF)], work, own_g, other_g, beside
    )
    grad_rows = lax.psum_scatter(partial, "dp", scatter_dimension=0, tiled=True).astype(F32)

    outs = halves_of(SHARDS * ROWS, width)
    beside_x = swap(jnp.concatenate([got_x, other_x], axis=0), 1)
    keep_y, send_y = call(
        forward_kernel, outs, 3 * work, got_x, other_x, beside_x, wg, wu, wd
    )
    keep_dx, send_dx = call(
        backward_kernel, outs, 3 * work, own_g, other_g, beside, wg, wu, wd
    )
    part_y = lax.ppermute(reduce_shards(keep_y, send_y), "pipe", onward)
    part_dx = reduce_shards(keep_dx, send_dx)

    back = jnp.concatenate([part_y, part_dx], axis=1).reshape(EXPERTS, SLOTS, -1)
    back = route(back).reshape(ROWS, -1)
    routed = combine(table_f, back[:, :width])
    grad_input = combine(table_b, back[:, width:])
    return (routed[None], grad_input[None], grad_rows[None])


def solution(mesh):
    token = P("pipe", ("expert", "dp"), None)
    in_specs = (
        token, token, token, token, token, token,
        P("pipe", ("expert", "dp"), None, None, None),
        P("pipe", None, "expert"),
        P("pipe", None, "expert"),
        P("pipe", "expert", None),
    )
    return jax.shard_map(
        on_device, mesh=mesh, in_specs=in_specs, out_specs=(token, token, token), check_vma=False
    )
```

time: 203 us -> 162 us (0.80)
  the two profiles are of different devices: /device:TPU:140 before, /device:TPU:1 now
where the time goes in v2:
time: 162 us; the launch traced here: 161 us
  blocking collectives  52 us (32%)
  starting transfers between devices  38.5 us (24%)
  waiting for transfers between devices  38.5 us (24%)
  between operations  14.4 us (9%)
  Pallas kernels  7.12 us (4%)
  local copies, waits for them, and re-layouts  6.86 us (4%)
  other arithmetic  2.31 us (1%)
  matrix products  1.8 us (1%)
    all_to_all x1, blocking collectives, route(): lax.all_to_all(rows, ('expert', 'dp'), split_axis=0, concat_axis=0, tiled...  52 us
    ppermute x8, starting transfers between devices, swap(): return lax.ppermute(rows, 'expert', [(i, i ^ bit) for i in range(count)])  29.6 us
    all_to_all x1, waiting for transfers between devices, route(): lax.all_to_all(rows, ('expert', 'dp'), split_axis=0, concat_axis=0, tiled...  15.6 us
    reduce_scatter x1, waiting for transfers between devices, on_device(): lax.psum_scatter(partial, 'dp', scatter_dimension=0, tiled=True).astype(F32)  11.1 us
    ppermute x8, waiting for transfers between devices, swap(): return lax.ppermute(rows, 'expert', [(i, i ^ bit) for i in range(count)])  7.4 us
    pallas_call x5, Pallas kernels, call(): pl.pallas_call(kernel, out_shape=tuple(outs), in_specs=[VMEM] * len(array...  5.69 us
    unnamed x18, local copies, waits for them, and re-layouts  4.37 us
    ppermute x1, waiting for transfers between devices, on_device(): part_y = lax.ppermute(reduce_shards(keep_y, send_y), 'pipe', onward)  4.35 us
  transfers between devices with their start and end apart: 12, of which 7 were waited for; matrix products, arithmetic and copies ran while one was open for 2% of the time, Pallas kernels for 4%

profile of v2, /device:TPU:1, one launch (start us, length us, event | category | flops | bytes accessed | tf_op | source)
XLA Modules:
  0.0 161.5 jit_solution(11680338221549325023)
XLA Ops:
  7.2 0.0 reduce-scatter.2.cloned.1.call-start
  7.3 0.9 reshape_squeeze.3.refs_6_
  8.2 0.1 pad_add_fusion.shard_ref
  8.2 0.0 copy-start.3
  8.2 0.8 copy-done.3
  9.0 0.0 copy-start.4
  9.0 0.8 copy-done.4
  9.9 0.0 copy-start.5
  9.9 0.7 copy-done.5
  10.5 0.0 copy-start.6
  10.5 0.7 copy-done.6
  11.2 0.0 copy-start.7
  11.2 0.7 copy-done.7
  11.9 0.0 copy-start.8
  11.9 0.7 copy-done.8
  12.6 1.4 build_rows.1
  14.0 0.2 reshape.18
  14.3 52.0 %all_to_all.10 = bf16[16,2,9216]{2,1,0:T(2,128)(2,1)S(1)} all-to-all(bf16[16,2,9216]{2,1,0:T(2,128)(2,1)S(1)} %reshape.18), channel_id=1, replica_groups={{0,16,32,48,72,88,104,120,131,147,163,179,203,219,235,251},{4,20,36,52,..., dimensions={0} | all-to-all | bytes 1179648 | tf_op jit(solution)/shard_map/all_to_all | solution.py:39
  66.3 0.2 reshape.19
  66.5 0.0 copy-start.2
  66.6 9.0 %collective-permute-start.1 = (bf16[32,3584]{1,0:T(8,128)(2,1)S(1)}, bf16[32,3584]{1,0:T(8,128)(2,1)S(1)}, u32[]{:S(2)}, u32[]{:S(2)}) collective-permute-start(bf16[32,3584]{1,0:T(8,128)(2,1)S(1)} %get-tuple-element.25.own), channel_id=1, source_target_pairs={{0,8},{4,12},{8,0},{12,4},{16,24},{20,28},{24,16},{28,20},{32,40},... | collective-permute-start | bytes 688136 | tf_op jit(solution)/shard_map/ppermute | solution.py:51
  75.6 0.0 copy-start.1
  75.7 0.0 copy-start
  75.7 2.2 %collective-permute-start.6 = (bf16[32,4608]{1,0:T(8,128)(2,1)S(1)}, bf16[32,4608]{1,0:T(8,128)(2,1)S(1)}, u32[]{:S(2)}, u32[]{:S(2)}) collective-permute-start(bf16[32,4608]{1,0:T(8,128)(2,1)S(1)} %pad_maximum_fusion.2), channel_id=1, source_target_pairs={{0,8},{4,12},{8,0},{12,4},{16,24},{20,28},{24,16},{28,20},{32,40},... | collective-permute-start | bytes 884744 | tf_op jit(solution)/shard_map/ppermute | solution.py:51
  77.9 2.1 %collective-permute-done.1.near = bf16[32,3584]{1,0:T(8,128)(2,1)S(1)} collective-permute-done((bf16[32,3584]{1,0:T(8,128)(2,1)S(1)}, bf16[32,3584]{1,0:T(8,128)(2,1)S(1)}, u32[]{:S(2)}, u32[]{:S(2)}) %collective-permute-start.1) | collective-permute-done | bytes 229408 | tf_op jit(solution)/shard_map/ppermute | solution.py:51
  80.1 5.3 %collective-permute-start.2 = (bf16[64,3584]{1,0:T(8,128)(2,1)S(1)}, bf16[64,3584]{1,0:T(8,128)(2,1)S(1)}, u32[]{:S(2)}, u32[]{:S(2)}) collective-permute-start(bf16[64,3584]{1,0:T(8,128)(2,1)S(1)} %pad_maximum_fusion), channel_id=1, source_target_pairs={{0,4},{4,0},{8,12},{12,8},{16,20},{20,16},{24,28},{28,24},{32,36},... | collective-permute-start | bytes 1376264 | tf_op jit(solution)/shard_map/ppermute | solution.py:51
  85.4 1.6 collective-permute-done.6.near
  87.0 3.4 %collective-permute-start.7 = (bf16[64,4096]{1,0:T(8,128)(2,1)S(1)}, bf16[64,4096]{1,0:T(8,128)(2,1)S(1)}, u32[]{:S(2)}, u32[]{:S(2)}) collective-permute-start(bf16[64,4096]{1,0:T(8,128)(2,1)S(1)} %fusion.5), channel_id=1, source_target_pairs={{0,4},{4,0},{8,12},{12,8},{16,20},{20,16},{24,28},{28,24},{32,36},... | collective-permute-start | bytes 1572872 | tf_op jit(solution)/shard_map/ppermute | solution.py:51
  90.5 0.0 collective-permute-done.2.beside
  90.5 0.0 copy-done.2
  90.5 0.0 copy-done.1
  90.5 0.0 copy-done
  90.5 1.0 forward_kernel.1
  91.5 1.9 %collective-permute-start.3 = (bf16[64,3584]{1,0:T(8,128)(2,1)S(1)}, bf16[64,3584]{1,0:T(8,128)(2,1)S(1)}, u32[]{:S(2)}, u32[]{:S(2)}) collective-permute-start(bf16[64,3584]{1,0:T(8,128)(2,1)S(1)} %get-tuple-element.17), channel_id=1, source_target_pairs={{0,4},{4,0},{8,12},{12,8},{16,20},{20,16},{24,28},{28,24},{32,36},... | collective-permute-start | bytes 1376264 | tf_op jit(solution)/shard_map/ppermute | solution.py:51
  93.5 0.0 collective-permute-done.7.beside
  93.5 2.6 %backward_kernel.1 = (f32[64,3584]{1,0:T(8,128)S(1)}, bf16[64,3584]{1,0:T(8,128)(2,1)S(1)}) custom-call(bf16[32,4608]{1,0:T(8,128)(2,1)S(1)} %slice.33.own, bf16[32,4608]{1,0:T(8,128)(2,1)S(1)} %collective-permute-done.6.near, bf16[64,4096]{1,0:T(8,128)(2,1)S(1)} %collective-permute-done.7.beside, bf16[3584,256]{1,0:T(8,128)(2,1)S(1)} %bitcast.29, ...), custom_call_target="tpu_custom_call" | custom-call | flops 704643072 | bytes 7995392 | tf_op jit(solution)/shard_map/backward_kernel/pallas_call | solution.py:156
  96.1 2.4 %collective-permute-start.8 = (bf16[64,3584]{1,0:T(8,128)(2,1)S(1)}, bf16[64,3584]{1,0:T(8,128)(2,1)S(1)}, u32[]{:S(2)}, u32[]{:S(2)}) collective-permute-start(bf16[64,3584]{1,0:T(8,128)(2,1)S(1)} %get-tuple-element.21), channel_id=1, source_target_pairs={{0,4},{4,0},{8,12},{12,8},{16,20},{20,16},{24,28},{28,24},{32,36},... | collective-permute-start | bytes 1376264 | tf_op jit(solution)/shard_map/ppermute | solution.py:51
  98.5 0.0 collective-permute-done.3.got_ref
  98.5 0.1 pair_kernel.2
  98.6 3.4 %collective-permute-start.4 = (bf16[32,3584]{1,0:T(8,128)(2,1)S(1)}, bf16[32,3584]{1,0:T(8,128)(2,1)S(1)}, u32[]{:S(2)}, u32[]{:S(2)}) collective-permute-start(bf16[32,3584]{1,0:T(8,128)(2,1)S(1)} %get-tuple-element.19), channel_id=1, source_target_pairs={{0,8},{4,12},{8,0},{12,4},{16,24},{20,28},{24,16},{28,20},{32,40},... | collective-permute-start | bytes 688136 | tf_op jit(solution)/shard_map/ppermute | solution.py:51
  102.0 1.9 %grad_kernel.1 = bf16[256,3584]{1,0:T(8,128)(2,1)} custom-call(bf16[32,4608]{1,0:T(8,128)(2,1)S(1)} %slice.33.own, bf16[32,4608]{1,0:T(8,128)(2,1)S(1)} %collective-permute-done.6.near, bf16[64,4096]{1,0:T(8,128)(2,1)S(1)} %collective-permute-done.7.beside), custom_call_target="tpu_custom_call" | custom-call | flops 234881024 | bytes 2949120 | tf_op jit(solution)/shard_map/grad_kernel/pallas_call | solution.py:156
  103.9 0.0 reduce-scatter.2.cloned.1.call-update
  103.9 0.0 collective-permute-done.8.got_ref
  103.9 0.1 pair_kernel.3
  104.0 1.9 %collective-permute-start.9 = (bf16[32,3584]{1,0:T(8,128)(2,1)S(1)}, bf16[32,3584]{1,0:T(8,128)(2,1)S(1)}, u32[]{:S(2)}, u32[]{:S(2)}) collective-permute-start(bf16[32,3584]{1,0:T(8,128)(2,1)S(1)} %get-tuple-element.23), channel_id=1, source_target_pairs={{0,8},{4,12},{8,0},{12,4},{16,24},{20,28},{24,16},{28,20},{32,40},... | collective-permute-start | bytes 688136 | tf_op jit(solution)/shard_map/ppermute | solution.py:51
  105.9 1.8 %collective-permute-done.4 = bf16[32,3584]{1,0:T(8,128)(2,1)S(1)} collective-permute-done((bf16[32,3584]{1,0:T(8,128)(2,1)S(1)}, bf16[32,3584]{1,0:T(8,128)(2,1)S(1)}, u32[]{:S(2)}, u32[]{:S(2)}) %collective-permute-start.4) | collective-permute-done | bytes 229408 | tf_op jit(solution)/shard_map/ppermute | solution.py:51
  107.8 3.1 %collective-permute-start.5 = (bf16[32,3584]{1,0:T(8,128)(2,1)S(1)}, bf16[32,3584]{1,0:T(8,128)(2,1)S(1)}, u32[]{:S(2)}, u32[]{:S(2)}) collective-permute-start(bf16[32,3584]{1,0:T(8,128)(2,1)S(1)} %add_convert_fusion.1), channel_id=1, source_target_pairs={{0,256},{256,512},{512,768},{768,0},{1,257},{257,513},{513,769},{7... | collective-permute-start | bytes 688136 | tf_op jit(solution)/shard_map/ppermute | solution.py:281
  110.9 1.9 %collective-permute-done.9 = bf16[32,3584]{1,0:T(8,128)(2,1)S(1)} collective-permute-done((bf16[32,3584]{1,0:T(8,128)(2,1)S(1)}, bf16[32,3584]{1,0:T(8,128)(2,1)S(1)}, u32[]{:S(2)}, u32[]{:S(2)}) %collective-permute-start.9) | collective-permute-done | bytes 229408 | tf_op jit(solution)/shard_map/ppermute | solution.py:51
  112.9 4.3 %collective-permute-done.5 = bf16[32,3584]{1,0:T(8,128)(2,1)S(1)} collective-permute-done((bf16[32,3584]{1,0:T(8,128)(2,1)S(1)}, bf16[32,3584]{1,0:T(8,128)(2,1)S(1)}, u32[]{:S(2)}, u32[]{:S(2)}) %collective-permute-start.5) | collective-permute-done | bytes 229408 | tf_op jit(solution)/shard_map/ppermute | solution.py:281
  117.2 0.9 reshape.20
  118.2 3.8 %all-to-all-start.1 = ((bf16[16,2,7168]{2,1,0:T(2,128)(2,1)}), bf16[16,2,7168]{2,1,0:T(2,128)(2,1)S(1)}, u32[]{:S(2)}, u32[]{:S(2)}) async-start(bf16[16,2,7168]{2,1,0:T(2,128)(2,1)} %reshape.20), calls=%async_computation.1 | async-start | bytes 917504 | tf_op jit(solution)/shard_map/all_to_all | solution.py:39
  122.0 1.9 %collective-permute-start = (f32[32,8]{1,0:T(8,128)S(1)}, f32[32,8]{1,0:T(8,128)S(1)}, u32[]{:S(2)}, u32[]{:S(2)}) collective-permute-start(f32[32,8]{1,0:T(8,128)S(1)} %get-tuple-element.14), channel_id=1, source_target_pairs={{0,256},{256,512},{512,768},{768,0},{1,257},{257,513},{513,769},{7... | collective-permute-start | bytes 3080 | tf_op jit(solution)/shard_map/ppermute | solution.py:256
  123.9 15.6 %all-to-all-done.1 = bf16[16,2,7168]{2,1,0:T(2,128)(2,1)S(1)} async-done(((bf16[16,2,7168]{2,1,0:T(2,128)(2,1)}), bf16[16,2,7168]{2,1,0:T(2,128)(2,1)S(1)}, u32[]{:S(2)}, u32[]{:S(2)}) %all-to-all-start.1) | async-done | bytes 458784 | tf_op jit(solution)/shard_map/all_to_all | solution.py:39
  139.6 0.2 reshape.21
  139.8 0.9 fusion.1
  140.7 0.0 collective-permute-done
  140.7 0.9 fusion
  141.6 11.1 %reduce-scatter.2.cloned.1.call-done = bf16[64,3584]{1,0:T(8,128)(2,1)} async-done(((bf16[256,3584]{1,0:T(8,128)(2,1)}), bf16[64,3584]{1,0:T(8,128)(2,1)}) %reduce-scatter.2.cloned.1.call-update) | async-done | bytes 458768 | tf_op jit(solution)/shard_map/reduce_scatter | solution.py:271
  152.6 2.0 %bitcast_convert_fusion = f32[1,64,3584]{2,1,0:T(8,128)} fusion(bf16[64,3584]{1,0:T(8,128)(2,1)} %reduce-scatter.2.cloned.1.call-done), kind=kLoop, calls=%fused_computation.14 | loop fusion | flops 229376 | bytes 1376256 | tf_op jit(solution)/shard_map/broadcast_in_dim | solution.py:288
  (10 shorter events, 0.3 us)
Async XLA Ops:
  7.2 145.5 %reduce-scatter.2.cloned.1.call-start = ((), (), s32[]{:S(2)}) async-start(), calls=%async_computation.3 | async-start | bytes 2293760 | tf_op jit(solution)/shard_map/reduce_scatter | solution.py:271
  8.2 0.8 copy-start.3
  9.0 0.8 copy-start.4
  9.9 0.7 copy-start.5
  10.5 0.7 copy-start.6
  11.2 0.7 copy-start.7
  11.9 0.7 copy-start.8
  66.5 24.0 %copy-start.2 = (bf16[1,256,3584]{2,1,0:T(8,128)(2,1)S(1)}, bf16[1,256,3584]{2,1,0:T(8,128)(2,1)}, u32[]{:S(2)}) copy-start(bf16[1,256,3584]{2,1,0:T(8,128)(2,1)} %param.19) | copy-start | bytes 5505028
  66.6 13.4 %collective-permute-start.1 = (bf16[32,3584]{1,0:T(8,128)(2,1)S(1)}, bf16[32,3584]{1,0:T(8,128)(2,1)S(1)}, u32[]{:S(2)}, u32[]{:S(2)}) collective-permute-start(bf16[32,3584]{1,0:T(8,128)(2,1)S(1)} %get-tuple-element.25.own), channel_id=1, source_target_pairs={{0,8},{4,12},{8,0},{12,4},{16,24},{20,28},{24,16},{28,20},{32,40},... | collective-permute-start | bytes 688136 | tf_op jit(solution)/shard_map/ppermute | solution.py:51
  75.6 14.9 %copy-start.1 = (bf16[1,3584,256]{2,1,0:T(8,128)(2,1)S(1)}, bf16[1,3584,256]{2,1,0:T(8,128)(2,1)}, u32[]{:S(2)}) copy-start(bf16[1,3584,256]{2,1,0:T(8,128)(2,1)} %param.18) | copy-start | bytes 5505028
  75.7 14.8 %copy-start = (bf16[1,3584,256]{2,1,0:T(8,128)(2,1)S(1)}, bf16[1,3584,256]{2,1,0:T(8,128)(2,1)}, u32[]{:S(2)}) copy-start(bf16[1,3584,256]{2,1,0:T(8,128)(2,1)} %param.17) | copy-start | bytes 5505028
  75.7 11.2 %collective-permute-start.6 = (bf16[32,4608]{1,0:T(8,128)(2,1)S(1)}, bf16[32,4608]{1,0:T(8,128)(2,1)S(1)}, u32[]{:S(2)}, u32[]{:S(2)}) collective-permute-start(bf16[32,4608]{1,0:T(8,128)(2,1)S(1)} %pad_maximum_fusion.2), channel_id=1, source_target_pairs={{0,8},{4,12},{8,0},{12,4},{16,24},{20,28},{24,16},{28,20},{32,40},... | collective-permute-start | bytes 884744 | tf_op jit(solution)/shard_map/ppermute | solution.py:51
  80.1 10.4 %collective-permute-start.2 = (bf16[64,3584]{1,0:T(8,128)(2,1)S(1)}, bf16[64,3584]{1,0:T(8,128)(2,1)S(1)}, u32[]{:S(2)}, u32[]{:S(2)}) collective-permute-start(bf16[64,3584]{1,0:T(8,128)(2,1)S(1)} %pad_maximum_fusion), channel_id=1, source_target_pairs={{0,4},{4,0},{8,12},{12,8},{16,20},{20,16},{24,28},{28,24},{32,36},... | collective-permute-start | bytes 1376264 | tf_op jit(solution)/shard_map/ppermute | solution.py:51
  87.0 6.4 %collective-permute-start.7 = (bf16[64,4096]{1,0:T(8,128)(2,1)S(1)}, bf16[64,4096]{1,0:T(8,128)(2,1)S(1)}, u32[]{:S(2)}, u32[]{:S(2)}) collective-permute-start(bf16[64,4096]{1,0:T(8,128)(2,1)S(1)} %fusion.5), channel_id=1, source_target_pairs={{0,4},{4,0},{8,12},{12,8},{16,20},{20,16},{24,28},{28,24},{32,36},... | collective-permute-start | bytes 1572872 | tf_op jit(solution)/shard_map/ppermute | solution.py:51
  91.5 7.0 %collective-permute-start.3 = (bf16[64,3584]{1,0:T(8,128)(2,1)S(1)}, bf16[64,3584]{1,0:T(8,128)(2,1)S(1)}, u32[]{:S(2)}, u32[]{:S(2)}) collective-permute-start(bf16[64,3584]{1,0:T(8,128)(2,1)S(1)} %get-tuple-element.17), channel_id=1, source_target_pairs={{0,4},{4,0},{8,12},{12,8},{16,20},{20,16},{24,28},{28,24},{32,36},... | collective-permute-start | bytes 1376264 | tf_op jit(solution)/shard_map/ppermute | solution.py:51
  96.1 7.8 %collective-permute-start.8 = (bf16[64,3584]{1,0:T(8,128)(2,1)S(1)}, bf16[64,3584]{1,0:T(8,128)(2,1)S(1)}, u32[]{:S(2)}, u32[]{:S(2)}) collective-permute-start(bf16[64,3584]{1,0:T(8,128)(2,1)S(1)} %get-tuple-element.21), channel_id=1, source_target_pairs={{0,4},{4,0},{8,12},{12,8},{16,20},{20,16},{24,28},{28,24},{32,36},... | collective-permute-start | bytes 1376264 | tf_op jit(solution)/shard_map/ppermute | solution.py:51
  98.6 9.1 %collective-permute-start.4 = (bf16[32,3584]{1,0:T(8,128)(2,1)S(1)}, bf16[32,3584]{1,0:T(8,128)(2,1)S(1)}, u32[]{:S(2)}, u32[]{:S(2)}) collective-permute-start(bf16[32,3584]{1,0:T(8,128)(2,1)S(1)} %get-tuple-element.19), channel_id=1, source_target_pairs={{0,8},{4,12},{8,0},{12,4},{16,24},{20,28},{24,16},{28,20},{32,40},... | collective-permute-start | bytes 688136 | tf_op jit(solution)/shard_map/ppermute | solution.py:51
  104.0 8.8 %collective-permute-start.9 = (bf16[32,3584]{1,0:T(8,128)(2,1)S(1)}, bf16[32,3584]{1,0:T(8,128)(2,1)S(1)}, u32[]{:S(2)}, u32[]{:S(2)}) collective-permute-start(bf16[32,3584]{1,0:T(8,128)(2,1)S(1)} %get-tuple-element.23), channel_id=1, source_target_pairs={{0,8},{4,12},{8,0},{12,4},{16,24},{20,28},{24,16},{28,20},{32,40},... | collective-permute-start | bytes 688136 | tf_op jit(solution)/shard_map/ppermute | solution.py:51
  107.8 9.4 %collective-permute-start.5 = (bf16[32,3584]{1,0:T(8,128)(2,1)S(1)}, bf16[32,3584]{1,0:T(8,128)(2,1)S(1)}, u32[]{:S(2)}, u32[]{:S(2)}) collective-permute-start(bf16[32,3584]{1,0:T(8,128)(2,1)S(1)} %add_convert_fusion.1), channel_id=1, source_target_pairs={{0,256},{256,512},{512,768},{768,0},{1,257},{257,513},{513,769},{7... | collective-permute-start | bytes 688136 | tf_op jit(solution)/shard_map/ppermute | solution.py:281
  118.2 21.4 %all-to-all-start.1 = ((bf16[16,2,7168]{2,1,0:T(2,128)(2,1)}), bf16[16,2,7168]{2,1,0:T(2,128)(2,1)S(1)}, u32[]{:S(2)}, u32[]{:S(2)}) async-start(bf16[16,2,7168]{2,1,0:T(2,128)(2,1)} %reshape.20), calls=%async_computation.1 | async-start | bytes 917504 | tf_op jit(solution)/shard_map/all_to_all | solution.py:39
  122.0 18.6 %collective-permute-start = (f32[32,8]{1,0:T(8,128)S(1)}, f32[32,8]{1,0:T(8,128)S(1)}, u32[]{:S(2)}, u32[]{:S(2)}) collective-permute-start(f32[32,8]{1,0:T(8,128)S(1)} %get-tuple-element.14), channel_id=1, source_target_pairs={{0,256},{256,512},{512,768},{768,0},{1,257},{257,513},{513,769},{7... | collective-permute-start | bytes 3080 | tf_op jit(solution)/shard_map/ppermute | solution.py:256
Sparse Core Ops, SparseCore 0:
  104.0 48.5 reduce-scatter.1

commit v3 on v2

--- a/solution.py
+++ b/solution.py
@@ -7,10 +7,12 @@
 from jax.experimental.pallas import tpu as pltpu
 from jax.sharding import PartitionSpec as P
 
+EXPERT = "expert"
 EXPERTS = 16
 SLOTS = 2
 SHARDS = 4
 ROWS = EXPERTS * SLOTS
+CHUNK = 512
 BF = jnp.bfloat16
 F32 = jnp.float32
 
@@ -68,7 +70,7 @@
     return jnp.dot(sel.astype(BF), rows, preferred_element_type=F32)
 
 
-def build_kernel(shard_ref, *refs):
+def build_kernel(*refs):
     hbm, (send_ref, wf_ref, tb_ref), held, sem = refs[:7], refs[7:10], refs[10:17], refs[17]
     copies = [
         pltpu.make_async_copy(src, dst, sem.at[i]) for i, (src, dst) in enumerate(zip(hbm, held))
@@ -78,67 +80,79 @@
     for copy in copies:
         copy.wait()
     ids_f, prob_f, x_ref, ids_b, prob_b, g_ref, pre_ref = held
-    width = g_ref.shape[1]
+
+    def store(at, rows):
+        size = rows.shape[1]
+        send_ref[:, :, at : at + size] = rows.reshape(EXPERTS, SLOTS, size).astype(BF)
+
+    tokens, width = g_ref.shape
     sel_b = selections(ids_b)
     both = functools.reduce(jnp.add, sel_b)
     scaled = functools.reduce(jnp.add, [s * prob_b[k : k + 1, :] for k, s in enumerate(sel_b)])
     scale = jnp.sum(scaled, axis=1, keepdims=True)
-    send_ref[:, :width] = (scale * pick(both, g_ref[...])).astype(BF)
-    chosen = len(sel_b)
-    hid = pre_ref.shape[1] // (2 * chosen)
+    for at in range(0, width, CHUNK):
+        store(at, scale * pick(both, g_ref[:, at : at + CHUNK]))
+    chosen, hid = pre_ref.shape[1], pre_ref.shape[3]
     units = hid // SHARDS
-    shard = shard_ref[0]
-    blocks = []
-    for step in range(SHARDS):
-        halves = []
-        for half in range(2):
-            part = jnp.zeros((ROWS, units), F32)
-            for k, sel in enumerate(sel_b):
-                start = (2 * k + half) * hid + (shard ^ step) * units
-                start = pl.multiple_of(start, 128)
-                part += pick(sel, pre_ref[:, pl.ds(start, units)])
-            halves.append(part)
-        blocks.append(halves)
+    index = lax.axis_index(EXPERT)
+    shard = index % SHARDS
+    count = 2 * tokens * chosen
+    column = lax.broadcasted_iota(jnp.int32, (tokens, count), 1)
+    token = lax.broadcasted_iota(jnp.int32, (tokens, count), 0)
+    rows = pre_ref[...].astype(F32).reshape(count, hid).astype(BF)
+    halves = []
+    for half in range(2):
+        sel = jnp.zeros((ROWS, count), F32)
+        for k, one in enumerate(sel_b):
+            spread = jnp.where(column == (token * chosen + k) * 2 + half, 1.0, 0.0)
+            sel += jnp.dot(one, spread, preferred_element_type=F32)
+        halves.append(pick(sel, rows))
+    blocks = [[h[:, s * units : (s + 1) * units] for h in halves] for s in range(SHARDS)]
     expert = lax.broadcasted_iota(jnp.int32, (ROWS, units), 0) // SLOTS
-    crosses = far_half(expert) != shard_ref[1]
+    crosses = far_half(expert) != far_half(index // SHARDS)
+    target = jnp.where(crosses, shard ^ 2, shard)
     for step in range(SHARDS):
         for half in range(2):
-            at = width + (2 * step + half) * units
-            part = jnp.where(crosses, blocks[step ^ 2][half], blocks[step][half])
-            send_ref[:, at : at + units] = part.astype(BF)
+            part = functools.reduce(
+                jnp.add,
+                [jnp.where((target ^ step) == s, blocks[s][half], 0.0) for s in range(SHARDS)],
+            )
+            store(width + (2 * step + half) * units, part)
     tb_ref[...] = both
     sel_f = selections(ids_f)
-    send_ref[:, width + 2 * hid :] = pick(functools.reduce(jnp.add, sel_f), x_ref[...]).astype(BF)
+    both = functools.reduce(jnp.add, sel_f)
+    for at in range(0, width, CHUNK):
+        store(width + 2 * hid + at, pick(both, x_ref[:, at : at + CHUNK]))
     wf_ref[...] = functools.reduce(
         jnp.add, [s * prob_f[k : k + 1, :] for k, s in enumerate(sel_f)]
     )
 
 
 VMEM = pl.BlockSpec(memory_space=pltpu.VMEM)
-
-
-def build_rows(place, *arrays):
+HBM = pl.BlockSpec(memory_space=pltpu.HBM)
+
+
+def build_rows(*arrays):
     x, pre = arrays[2], arrays[6]
     tokens, width = x.shape
-    total = 2 * width + pre.shape[1] // 2
+    total = 2 * width + 2 * pre.shape[3]
     return pl.pallas_call(
         build_kernel,
         out_shape=(
-            jax.ShapeDtypeStruct((ROWS, total), BF),
+            jax.ShapeDtypeStruct((EXPERTS, SLOTS, total), BF),
             jax.ShapeDtypeStruct((ROWS, tokens), F32),
             jax.ShapeDtypeStruct((ROWS, tokens), F32),
         ),
-        in_specs=[pl.BlockSpec(memory_space=pltpu.SMEM)]
-        + [pl.BlockSpec(memory_space=pl.ANY)] * len(arrays),
+        in_specs=[HBM] * len(arrays),
         out_specs=(VMEM,) * 3,
         scratch_shapes=[pltpu.VMEM(a.shape, a.dtype) for a in arrays]
         + [pltpu.SemaphoreType.DMA((len(arrays),))],
         cost_estimate=pl.CostEstimate(
             flops=4 * ROWS * tokens * width, bytes_accessed=2 << 20, transcendentals=0
         ),
-        compiler_params=pltpu.CompilerParams(vmem_limit_bytes=48 << 20),
+        compiler_params=pltpu.CompilerParams(vmem_limit_bytes=56 << 20),
         name="build_rows",
-    )(place, *arrays)
+    )(*arrays)
 
 
 def silu_pair(value):
@@ -147,7 +161,6 @@
 
 
 CONTRACT = (((1,), (1,)), ((), ()))
-CHUNK = 512
 
 
 def call(kernel, outs, flops, *arrays):
@@ -245,17 +258,15 @@
     tokens, width = x_fwd.shape[1:]
     wg, wu, wd = w_gate[0], w_up[0], w_down[0]
     units = wg.shape[1]
-    index = lax.axis_index("expert")
-    place = jnp.stack([index % SHARDS, far_half(index // SHARDS)]).astype(jnp.int32)
     send, table_f, table_b = build_rows(
-        place, ids_fwd[0].T, prob_fwd[0].T, x_fwd[0], ids_bwd[0].T, prob_bwd[0].T, grad_bwd[0],
-        pre_bwd[0].reshape(tokens, -1),
+        ids_fwd[0].T, prob_fwd[0].T, x_fwd[0], ids_bwd[0].T, prob_bwd[0].T, grad_bwd[0],
+        pre_bwd[0],
     )
     sections = lax.axis_size("pipe")
     onward = [(i, (i + 1) % sections) for i in range(sections)]
     table_f = lax.ppermute(table_f, "pipe", onward)
 
-    got = route(send.reshape(EXPERTS, SLOTS, -1)).reshape(ROWS, -1)
+    got = route(send).reshape(ROWS, -1)
     pair, near, far, end = width + 2 * units, width + 4 * units, width + 6 * units, width + 8 * units
     other_g = swap(jnp.concatenate([got[:, :width], got[:, near:end]], axis=1), 2)
     got_x = got[:, end:]

time: 162 us -> 159 us (0.981)
  local copies, waits for them, and re-layouts: 6.86 us -> 1.42 us
  Pallas kernels: 7.12 us -> 8.74 us
    unnamed x18 -> x10, local copies, waits for them, and re-layouts: 4.37 us -> 0.03 us
where the time goes in v3:
time: 159 us; the launch traced here: 158 us
  blocking collectives  52.2 us (33%)
  starting transfers between devices  38.5 us (24%)
  waiting for transfers between devices  38.5 us (24%)
  between operations  14.3 us (9%)
  Pallas kernels  8.74 us (5%)
  other arithmetic  2.23 us (1%)
  matrix products  1.8 us (1%)
    all_to_all x1, blocking collectives, route(): lax.all_to_all(rows, ('expert', 'dp'), split_axis=0, concat_axis=0, tiled...  52.2 us
    ppermute x8, starting transfers between devices, swap(): return lax.ppermute(rows, 'expert', [(i, i ^ bit) for i in range(count)])  29.6 us
    all_to_all x1, waiting for transfers between devices, route(): lax.all_to_all(rows, ('expert', 'dp'), split_axis=0, concat_axis=0, tiled...  15.4 us
    reduce_scatter x1, waiting for transfers between devices, on_device(): lax.psum_scatter(partial, 'dp', scatter_dimension=0, tiled=True).astype(F32)  11.3 us
    ppermute x8, waiting for transfers between devices, swap(): return lax.ppermute(rows, 'expert', [(i, i ^ bit) for i in range(count)])  7.43 us
    pallas_call x5, Pallas kernels, call(): pl.pallas_call(kernel, out_shape=tuple(outs), in_specs=[VMEM] * len(array...  5.7 us
    ppermute x1, waiting for transfers between devices, on_device(): part_y = lax.ppermute(reduce_shards(keep_y, send_y), 'pipe', onward)  4.32 us
    all_to_all x1, starting transfers between devices, route(): lax.all_to_all(rows, ('expert', 'dp'), split_axis=0, concat_axis=0, tiled...  3.8 us
  transfers between devices with their start and end apart: 12, of which 7 were waited for; matrix products, arithmetic and copies ran while one was open for 2% of the time, Pallas kernels for 4%

profile of v3, /device:TPU:1, one launch (start us, length us, event | category | flops | bytes accessed | tf_op | source)
XLA Modules:
  0.0 157.7 jit_solution(928175930895805054)
XLA Ops:
  7.2 0.0 reduce-scatter.2.cloned.1.call-start
  7.2 3.0 %build_rows.1 = (bf16[16,2,9216]{2,1,0:T(2,128)(2,1)}, f32[32,8]{1,0:T(8,128)}, f32[32,8]{1,0:T(8,128)}) custom-call(s32[2,8]{1,0:T(2,128)} %bitcast.36, f32[2,8]{1,0:T(2,128)} %bitcast.37, bf16[8,3584]{1,0:T(8,128)(2,1)} %bitcast.34, s32[2,8]{1,0:T(2,128)} %bitcast.38, f32[2,8]{1,0:T(2,128)} %bitcast.39, bf16[8,3584]{1,0:T(8,128)(2,1)} %bitcast.35, ...), custom_call_target="tpu_custom_call" | custom-call | flops 3670016 | bytes 2097152 | tf_op jit(solution)/shard_map/build_rows/pallas_call | solution.py:139
  10.3 52.2 %all_to_all.10 = bf16[16,2,9216]{2,1,0:T(2,128)(2,1)S(1)} all-to-all(bf16[16,2,9216]{2,1,0:T(2,128)(2,1)} %get-tuple-element.15), channel_id=1, replica_groups={{0,16,32,48,72,88,104,120,131,147,163,179,203,219,235,251},{4,20,36,52,..., dimensions={0} | all-to-all | bytes 1179648 | tf_op jit(solution)/shard_map/all_to_all | solution.py:41
  62.5 0.2 reshape.15
  62.7 0.0 copy-start.2
  62.8 9.1 %collective-permute-start.1 = (bf16[32,3584]{1,0:T(8,128)(2,1)S(1)}, bf16[32,3584]{1,0:T(8,128)(2,1)S(1)}, u32[]{:S(2)}, u32[]{:S(2)}) collective-permute-start(bf16[32,3584]{1,0:T(8,128)(2,1)S(1)} %get-tuple-element.25.own), channel_id=1, source_target_pairs={{0,8},{4,12},{8,0},{12,4},{16,24},{20,28},{24,16},{28,20},{32,40},... | collective-permute-start | bytes 688136 | tf_op jit(solution)/shard_map/ppermute | solution.py:53
  71.9 0.0 copy-start.1
  71.9 0.0 copy-start
  71.9 2.2 %collective-permute-start.6 = (bf16[32,4608]{1,0:T(8,128)(2,1)S(1)}, bf16[32,4608]{1,0:T(8,128)(2,1)S(1)}, u32[]{:S(2)}, u32[]{:S(2)}) collective-permute-start(bf16[32,4608]{1,0:T(8,128)(2,1)S(1)} %pad_maximum_fusion.2), channel_id=1, source_target_pairs={{0,8},{4,12},{8,0},{12,4},{16,24},{20,28},{24,16},{28,20},{32,40},... | collective-permute-start | bytes 884744 | tf_op jit(solution)/shard_map/ppermute | solution.py:53
  74.1 2.2 %collective-permute-done.1.near = bf16[32,3584]{1,0:T(8,128)(2,1)S(1)} collective-permute-done((bf16[32,3584]{1,0:T(8,128)(2,1)S(1)}, bf16[32,3584]{1,0:T(8,128)(2,1)S(1)}, u32[]{:S(2)}, u32[]{:S(2)}) %collective-permute-start.1) | collective-permute-done | bytes 229408 | tf_op jit(solution)/shard_map/ppermute | solution.py:53
  76.3 5.3 %collective-permute-start.2 = (bf16[64,3584]{1,0:T(8,128)(2,1)S(1)}, bf16[64,3584]{1,0:T(8,128)(2,1)S(1)}, u32[]{:S(2)}, u32[]{:S(2)}) collective-permute-start(bf16[64,3584]{1,0:T(8,128)(2,1)S(1)} %pad_maximum_fusion), channel_id=1, source_target_pairs={{0,4},{4,0},{8,12},{12,8},{16,20},{20,16},{24,28},{28,24},{32,36},... | collective-permute-start | bytes 1376264 | tf_op jit(solution)/shard_map/ppermute | solution.py:53
  81.6 1.6 %collective-permute-done.6.near = bf16[32,4608]{1,0:T(8,128)(2,1)S(1)} collective-permute-done((bf16[32,4608]{1,0:T(8,128)(2,1)S(1)}, bf16[32,4608]{1,0:T(8,128)(2,1)S(1)}, u32[]{:S(2)}, u32[]{:S(2)}) %collective-permute-start.6) | collective-permute-done | bytes 294944 | tf_op jit(solution)/shard_map/ppermute | solution.py:53
  83.3 3.4 %collective-permute-start.7 = (bf16[64,4096]{1,0:T(8,128)(2,1)S(1)}, bf16[64,4096]{1,0:T(8,128)(2,1)S(1)}, u32[]{:S(2)}, u32[]{:S(2)}) collective-permute-start(bf16[64,4096]{1,0:T(8,128)(2,1)S(1)} %fusion.5), channel_id=1, source_target_pairs={{0,4},{4,0},{8,12},{12,8},{16,20},{20,16},{24,28},{28,24},{32,36},... | collective-permute-start | bytes 1572872 | tf_op jit(solution)/shard_map/ppermute | solution.py:53
  86.7 0.0 collective-permute-done.2.beside
  86.7 0.0 copy-done.2
  86.7 0.0 copy-done.1
  86.7 0.0 copy-done
  86.8 1.0 forward_kernel.1
  87.8 1.9 %collective-permute-start.3 = (bf16[64,3584]{1,0:T(8,128)(2,1)S(1)}, bf16[64,3584]{1,0:T(8,128)(2,1)S(1)}, u32[]{:S(2)}, u32[]{:S(2)}) collective-permute-start(bf16[64,3584]{1,0:T(8,128)(2,1)S(1)} %get-tuple-element.17), channel_id=1, source_target_pairs={{0,4},{4,0},{8,12},{12,8},{16,20},{20,16},{24,28},{28,24},{32,36},... | collective-permute-start | bytes 1376264 | tf_op jit(solution)/shard_map/ppermute | solution.py:53
  89.7 0.0 collective-permute-done.7.beside
  89.7 2.6 %backward_kernel.1 = (f32[64,3584]{1,0:T(8,128)S(1)}, bf16[64,3584]{1,0:T(8,128)(2,1)S(1)}) custom-call(bf16[32,4608]{1,0:T(8,128)(2,1)S(1)} %slice.33.own, bf16[32,4608]{1,0:T(8,128)(2,1)S(1)} %collective-permute-done.6.near, bf16[64,4096]{1,0:T(8,128)(2,1)S(1)} %collective-permute-done.7.beside, bf16[3584,256]{1,0:T(8,128)(2,1)S(1)} %bitcast.28, ...), custom_call_target="tpu_custom_call" | custom-call | flops 704643072 | bytes 7995392 | tf_op jit(solution)/shard_map/backward_kernel/pallas_call | solution.py:169
  92.3 2.4 %collective-permute-start.8 = (bf16[64,3584]{1,0:T(8,128)(2,1)S(1)}, bf16[64,3584]{1,0:T(8,128)(2,1)S(1)}, u32[]{:S(2)}, u32[]{:S(2)}) collective-permute-start(bf16[64,3584]{1,0:T(8,128)(2,1)S(1)} %get-tuple-element.21), channel_id=1, source_target_pairs={{0,4},{4,0},{8,12},{12,8},{16,20},{20,16},{24,28},{28,24},{32,36},... | collective-permute-start | bytes 1376264 | tf_op jit(solution)/shard_map/ppermute | solution.py:53
  94.7 0.0 collective-permute-done.3.got_ref
  94.7 0.1 pair_kernel.2
  94.8 3.4 %collective-permute-start.4 = (bf16[32,3584]{1,0:T(8,128)(2,1)S(1)}, bf16[32,3584]{1,0:T(8,128)(2,1)S(1)}, u32[]{:S(2)}, u32[]{:S(2)}) collective-permute-start(bf16[32,3584]{1,0:T(8,128)(2,1)S(1)} %get-tuple-element.19), channel_id=1, source_target_pairs={{0,8},{4,12},{8,0},{12,4},{16,24},{20,28},{24,16},{28,20},{32,40},... | collective-permute-start | bytes 688136 | tf_op jit(solution)/shard_map/ppermute | solution.py:53
  98.2 1.9 %grad_kernel.1 = bf16[256,3584]{1,0:T(8,128)(2,1)} custom-call(bf16[32,4608]{1,0:T(8,128)(2,1)S(1)} %slice.33.own, bf16[32,4608]{1,0:T(8,128)(2,1)S(1)} %collective-permute-done.6.near, bf16[64,4096]{1,0:T(8,128)(2,1)S(1)} %collective-permute-done.7.beside), custom_call_target="tpu_custom_call" | custom-call | flops 234881024 | bytes 2949120 | tf_op jit(solution)/shard_map/grad_kernel/pallas_call | solution.py:169
  100.1 0.0 reduce-scatter.2.cloned.1.call-update
  100.2 0.0 collective-permute-done.8.got_ref
  100.2 0.1 pair_kernel.3
  100.3 1.9 %collective-permute-start.9 = (bf16[32,3584]{1,0:T(8,128)(2,1)S(1)}, bf16[32,3584]{1,0:T(8,128)(2,1)S(1)}, u32[]{:S(2)}, u32[]{:S(2)}) collective-permute-start(bf16[32,3584]{1,0:T(8,128)(2,1)S(1)} %get-tuple-element.23), channel_id=1, source_target_pairs={{0,8},{4,12},{8,0},{12,4},{16,24},{20,28},{24,16},{28,20},{32,40},... | collective-permute-start | bytes 688136 | tf_op jit(solution)/shard_map/ppermute | solution.py:53
  102.2 1.8 %collective-permute-done.4 = bf16[32,3584]{1,0:T(8,128)(2,1)S(1)} collective-permute-done((bf16[32,3584]{1,0:T(8,128)(2,1)S(1)}, bf16[32,3584]{1,0:T(8,128)(2,1)S(1)}, u32[]{:S(2)}, u32[]{:S(2)}) %collective-permute-start.4) | collective-permute-done | bytes 229408 | tf_op jit(solution)/shard_map/ppermute | solution.py:53
  104.0 3.2 %collective-permute-start.5 = (bf16[32,3584]{1,0:T(8,128)(2,1)S(1)}, bf16[32,3584]{1,0:T(8,128)(2,1)S(1)}, u32[]{:S(2)}, u32[]{:S(2)}) collective-permute-start(bf16[32,3584]{1,0:T(8,128)(2,1)S(1)} %add_convert_fusion.1), channel_id=1, source_target_pairs={{0,256},{256,512},{512,768},{768,0},{1,257},{257,513},{513,769},{7... | collective-permute-start | bytes 688136 | tf_op jit(solution)/shard_map/ppermute | solution.py:292
  107.2 1.9 %collective-permute-done.9 = bf16[32,3584]{1,0:T(8,128)(2,1)S(1)} collective-permute-done((bf16[32,3584]{1,0:T(8,128)(2,1)S(1)}, bf16[32,3584]{1,0:T(8,128)(2,1)S(1)}, u32[]{:S(2)}, u32[]{:S(2)}) %collective-permute-start.9) | collective-permute-done | bytes 229408 | tf_op jit(solution)/shard_map/ppermute | solution.py:53
  109.1 0.0 copy-start.4
  109.1 0.0 copy-start.3
  109.1 4.3 %collective-permute-done.5 = bf16[32,3584]{1,0:T(8,128)(2,1)S(1)} collective-permute-done((bf16[32,3584]{1,0:T(8,128)(2,1)S(1)}, bf16[32,3584]{1,0:T(8,128)(2,1)S(1)}, u32[]{:S(2)}, u32[]{:S(2)}) %collective-permute-start.5) | collective-permute-done | bytes 229408 | tf_op jit(solution)/shard_map/ppermute | solution.py:292
  113.5 0.9 reshape.16
  114.4 3.8 %all-to-all-start.1 = ((bf16[16,2,7168]{2,1,0:T(2,128)(2,1)}), bf16[16,2,7168]{2,1,0:T(2,128)(2,1)S(1)}, u32[]{:S(2)}, u32[]{:S(2)}) async-start(bf16[16,2,7168]{2,1,0:T(2,128)(2,1)} %reshape.16), calls=%async_computation.1 | async-start | bytes 917504 | tf_op jit(solution)/shard_map/all_to_all | solution.py:41
  118.2 0.0 copy-done.4
  118.2 1.9 %collective-permute-start = (f32[32,8]{1,0:T(8,128)S(1)}, f32[32,8]{1,0:T(8,128)S(1)}, u32[]{:S(2)}, u32[]{:S(2)}) collective-permute-start(f32[32,8]{1,0:T(8,128)S(1)} %copy-done.4), channel_id=1, source_target_pairs={{0,256},{256,512},{512,768},{768,0},{1,257},{257,513},{513,769},{7... | collective-permute-start | bytes 3080 | tf_op jit(solution)/shard_map/ppermute | solution.py:267
  120.2 15.4 %all-to-all-done.1 = bf16[16,2,7168]{2,1,0:T(2,128)(2,1)S(1)} async-done(((bf16[16,2,7168]{2,1,0:T(2,128)(2,1)}), bf16[16,2,7168]{2,1,0:T(2,128)(2,1)S(1)}, u32[]{:S(2)}, u32[]{:S(2)}) %all-to-all-start.1) | async-done | bytes 458784 | tf_op jit(solution)/shard_map/all_to_all | solution.py:41
  135.6 0.2 reshape.17
  135.8 0.0 copy-done.3
  135.8 0.9 fusion.1
  136.7 0.0 collective-permute-done
  136.7 0.9 fusion
  137.6 11.3 %reduce-scatter.2.cloned.1.call-done = bf16[64,3584]{1,0:T(8,128)(2,1)} async-done(((bf16[256,3584]{1,0:T(8,128)(2,1)}), bf16[64,3584]{1,0:T(8,128)(2,1)}) %reduce-scatter.2.cloned.1.call-update) | async-done | bytes 458768 | tf_op jit(solution)/shard_map/reduce_scatter | solution.py:282
  148.9 2.0 %bitcast_convert_fusion = f32[1,64,3584]{2,1,0:T(8,128)} fusion(bf16[64,3584]{1,0:T(8,128)(2,1)} %reduce-scatter.2.cloned.1.call-done), kind=kLoop, calls=%fused_computation.14 | loop fusion | flops 229376 | bytes 1376256 | tf_op jit(solution)/shard_map/broadcast_in_dim | solution.py:299
  (10 shorter events, 0.3 us)
Async XLA Ops:
  7.2 141.7 %reduce-scatter.2.cloned.1.call-start = ((), (), s32[]{:S(2)}) async-start(), calls=%async_computation.3 | async-start | bytes 2293760 | tf_op jit(solution)/shard_map/reduce_scatter | solution.py:282
  62.7 24.0 %copy-start.2 = (bf16[1,256,3584]{2,1,0:T(8,128)(2,1)S(1)}, bf16[1,256,3584]{2,1,0:T(8,128)(2,1)}, u32[]{:S(2)}) copy-start(bf16[1,256,3584]{2,1,0:T(8,128)(2,1)} %param.19) | copy-start | bytes 5505028
  62.8 13.5 %collective-permute-start.1 = (bf16[32,3584]{1,0:T(8,128)(2,1)S(1)}, bf16[32,3584]{1,0:T(8,128)(2,1)S(1)}, u32[]{:S(2)}, u32[]{:S(2)}) collective-permute-start(bf16[32,3584]{1,0:T(8,128)(2,1)S(1)} %get-tuple-element.25.own), channel_id=1, source_target_pairs={{0,8},{4,12},{8,0},{12,4},{16,24},{20,28},{24,16},{28,20},{32,40},... | collective-permute-start | bytes 688136 | tf_op jit(solution)/shard_map/ppermute | solution.py:53
  71.9 14.9 %copy-start.1 = (bf16[1,3584,256]{2,1,0:T(8,128)(2,1)S(1)}, bf16[1,3584,256]{2,1,0:T(8,128)(2,1)}, u32[]{:S(2)}) copy-start(bf16[1,3584,256]{2,1,0:T(8,128)(2,1)} %param.18) | copy-start | bytes 5505028
  71.9 14.8 %copy-start = (bf16[1,3584,256]{2,1,0:T(8,128)(2,1)S(1)}, bf16[1,3584,256]{2,1,0:T(8,128)(2,1)}, u32[]{:S(2)}) copy-start(bf16[1,3584,256]{2,1,0:T(8,128)(2,1)} %param.17) | copy-start | bytes 5505028
  71.9 11.2 %collective-permute-start.6 = (bf16[32,4608]{1,0:T(8,128)(2,1)S(1)}, bf16[32,4608]{1,0:T(8,128)(2,1)S(1)}, u32[]{:S(2)}, u32[]{:S(2)}) collective-permute-start(bf16[32,4608]{1,0:T(8,128)(2,1)S(1)} %pad_maximum_fusion.2), channel_id=1, source_target_pairs={{0,8},{4,12},{8,0},{12,4},{16,24},{20,28},{24,16},{28,20},{32,40},... | collective-permute-start | bytes 884744 | tf_op jit(solution)/shard_map/ppermute | solution.py:53
  76.3 10.4 %collective-permute-start.2 = (bf16[64,3584]{1,0:T(8,128)(2,1)S(1)}, bf16[64,3584]{1,0:T(8,128)(2,1)S(1)}, u32[]{:S(2)}, u32[]{:S(2)}) collective-permute-start(bf16[64,3584]{1,0:T(8,128)(2,1)S(1)} %pad_maximum_fusion), channel_id=1, source_target_pairs={{0,4},{4,0},{8,12},{12,8},{16,20},{20,16},{24,28},{28,24},{32,36},... | collective-permute-start | bytes 1376264 | tf_op jit(solution)/shard_map/ppermute | solution.py:53
  83.3 6.4 %collective-permute-start.7 = (bf16[64,4096]{1,0:T(8,128)(2,1)S(1)}, bf16[64,4096]{1,0:T(8,128)(2,1)S(1)}, u32[]{:S(2)}, u32[]{:S(2)}) collective-permute-start(bf16[64,4096]{1,0:T(8,128)(2,1)S(1)} %fusion.5), channel_id=1, source_target_pairs={{0,4},{4,0},{8,12},{12,8},{16,20},{20,16},{24,28},{28,24},{32,36},... | collective-permute-start | bytes 1572872 | tf_op jit(solution)/shard_map/ppermute | solution.py:53
  87.8 7.0 %collective-permute-start.3 = (bf16[64,3584]{1,0:T(8,128)(2,1)S(1)}, bf16[64,3584]{1,0:T(8,128)(2,1)S(1)}, u32[]{:S(2)}, u32[]{:S(2)}) collective-permute-start(bf16[64,3584]{1,0:T(8,128)(2,1)S(1)} %get-tuple-element.17), channel_id=1, source_target_pairs={{0,4},{4,0},{8,12},{12,8},{16,20},{20,16},{24,28},{28,24},{32,36},... | collective-permute-start | bytes 1376264 | tf_op jit(solution)/shard_map/ppermute | solution.py:53
  92.3 7.9 %collective-permute-start.8 = (bf16[64,3584]{1,0:T(8,128)(2,1)S(1)}, bf16[64,3584]{1,0:T(8,128)(2,1)S(1)}, u32[]{:S(2)}, u32[]{:S(2)}) collective-permute-start(bf16[64,3584]{1,0:T(8,128)(2,1)S(1)} %get-tuple-element.21), channel_id=1, source_target_pairs={{0,4},{4,0},{8,12},{12,8},{16,20},{20,16},{24,28},{28,24},{32,36},... | collective-permute-start | bytes 1376264 | tf_op jit(solution)/shard_map/ppermute | solution.py:53
  94.8 9.1 %collective-permute-start.4 = (bf16[32,3584]{1,0:T(8,128)(2,1)S(1)}, bf16[32,3584]{1,0:T(8,128)(2,1)S(1)}, u32[]{:S(2)}, u32[]{:S(2)}) collective-permute-start(bf16[32,3584]{1,0:T(8,128)(2,1)S(1)} %get-tuple-element.19), channel_id=1, source_target_pairs={{0,8},{4,12},{8,0},{12,4},{16,24},{20,28},{24,16},{28,20},{32,40},... | collective-permute-start | bytes 688136 | tf_op jit(solution)/shard_map/ppermute | solution.py:53
  100.3 8.8 %collective-permute-start.9 = (bf16[32,3584]{1,0:T(8,128)(2,1)S(1)}, bf16[32,3584]{1,0:T(8,128)(2,1)S(1)}, u32[]{:S(2)}, u32[]{:S(2)}) collective-permute-start(bf16[32,3584]{1,0:T(8,128)(2,1)S(1)} %get-tuple-element.23), channel_id=1, source_target_pairs={{0,8},{4,12},{8,0},{12,4},{16,24},{20,28},{24,16},{28,20},{32,40},... | collective-permute-start | bytes 688136 | tf_op jit(solution)/shard_map/ppermute | solution.py:53
  104.0 9.4 %collective-permute-start.5 = (bf16[32,3584]{1,0:T(8,128)(2,1)S(1)}, bf16[32,3584]{1,0:T(8,128)(2,1)S(1)}, u32[]{:S(2)}, u32[]{:S(2)}) collective-permute-start(bf16[32,3584]{1,0:T(8,128)(2,1)S(1)} %add_convert_fusion.1), channel_id=1, source_target_pairs={{0,256},{256,512},{512,768},{768,0},{1,257},{257,513},{513,769},{7... | collective-permute-start | bytes 688136 | tf_op jit(solution)/shard_map/ppermute | solution.py:292
  109.1 9.2 %copy-start.4 = (f32[32,8]{1,0:T(8,128)S(1)}, f32[32,8]{1,0:T(8,128)}, u32[]{:S(2)}) copy-start(f32[32,8]{1,0:T(8,128)} %get-tuple-element.14) | copy-start | bytes 3076
  109.1 26.7 %copy-start.3 = (f32[32,8]{1,0:T(8,128)S(1)}, f32[32,8]{1,0:T(8,128)}, u32[]{:S(2)}) copy-start(f32[32,8]{1,0:T(8,128)} %get-tuple-element.24) | copy-start | bytes 3076
  114.4 21.2 %all-to-all-start.1 = ((bf16[16,2,7168]{2,1,0:T(2,128)(2,1)}), bf16[16,2,7168]{2,1,0:T(2,128)(2,1)S(1)}, u32[]{:S(2)}, u32[]{:S(2)}) async-start(bf16[16,2,7168]{2,1,0:T(2,128)(2,1)} %reshape.16), calls=%async_computation.1 | async-start | bytes 917504 | tf_op jit(solution)/shard_map/all_to_all | solution.py:41
  118.2 18.5 %collective-permute-start = (f32[32,8]{1,0:T(8,128)S(1)}, f32[32,8]{1,0:T(8,128)S(1)}, u32[]{:S(2)}, u32[]{:S(2)}) collective-permute-start(f32[32,8]{1,0:T(8,128)S(1)} %copy-done.4), channel_id=1, source_target_pairs={{0,256},{256,512},{512,768},{768,0},{1,257},{257,513},{513,769},{7... | collective-permute-start | bytes 3080 | tf_op jit(solution)/shard_map/ppermute | solution.py:267
Sparse Core Ops, SparseCore 0:
  100.3 48.5 reduce-scatter.1
